TPU v7x, 32 devices: a whole 2x2x4 slice. The times are simulated.
32 devices in a mesh: gx: 8 (over z, x), gy: 4 (over y, core).
Axes of the slice: x: 2, y: 2, z: 4, core: 2. Of those that a mesh axis runs over, the one named last changes fastest.
Arguments:
- theta: float32 [80, 512, 512], P(None, 'gx', 'gy'), may hold values from -6 to 6
- wind_u: float32 [80, 512, 512], P(None, 'gx', 'gy'), may hold values from -1 to 1
- wind_v: float32 [80, 512, 512], P(None, 'gx', 'gy'), may hold values from -1 to 1
- level_set: float32 [8, 4, 16, 128, 128], P('gx', 'gy'), may hold values from -6 to 6
- fuel_load: float32 [8, 4, 16, 128, 128], P('gx', 'gy'), may hold values from 0.5 to 1.5
- spread_base: float32 [8, 4, 16, 128, 128], P('gx', 'gy'), may hold values from 0.3 to 3
- tile_owner: int32 [8, 4, 16], P('gx', 'gy'), may hold values from 0 to 7, as said below
- tile_place: int32 [8, 4, 16], P('gx', 'gy'), may hold values from 0 to 511, as said below
Outputs:
- theta_next: float32 [80, 512, 512], P(None, 'gx', 'gy')
- level_next: float32 [8, 4, 16, 128, 128], P('gx', 'gy')
- fuel_next: float32 [8, 4, 16, 128, 128], P('gx', 'gy')
Inputs may be any that keep to these rules, and one draw needn't show every extreme that they name: Every tile of device (i, j) lies in the block of a device (tile_owner, j) of the same gy index; at most 2 tiles of one device lie in one owner's block, and in every draw some owner of each gy index holds exactly 2 tiles from every device of that index. `tile_place`: no two computed tiles have the same owner and place.
All inputs are finite; a program needn't handle non-finite values.
Results may differ from a plain program's by a relative error of at most 0.0003.
Values sent between devices are 32-bit elements; how exact they have to be, the bound alone decides.
A program may use at most 128 MiB of HBM per device.

v0:
```python
import jax
import jax.numpy as jnp
from jax import lax
from jax.sharding import PartitionSpec as P

LZ = 80
TA = 4
R = 32
KSUB = 6
CAP = 2
TPD = 16
S = 128


time_step = 0.03
diffusion = 0.15
burn_rate = 0.15
sharpness = 2.0
regular = 0.01
courant = 0.4
heat_gain = 2.0


def padded_2(cells, sides, width):
    for axis, dim in sides:
        count = lax.axis_size(axis)
        ends = count - 1
        head = lax.slice_in_dim(cells, 0, width, axis=dim)
        tail = lax.slice_in_dim(cells, cells.shape[dim] - width, cells.shape[dim], axis=dim)
        cells = jnp.concatenate(
            [
                lax.ppermute(tail, axis, [(i, (i + 1) % count) for i in range(ends)]),
                cells,
                lax.ppermute(head, axis, [((i + 1) % count, i) for i in range(ends)]),
            ],
            axis=dim,
        )
    return cells


def interp_table():
    where_fine = (jnp.arange(S, dtype=jnp.float32) + 0.5) / R + 0.5
    columns = jnp.arange(TA + 2, dtype=jnp.float32)
    return jnp.maximum(0.0, 1.0 - jnp.abs(where_fine[:, None] - columns[None, :]))


def average_table():
    block_of = jnp.arange(S, dtype=jnp.int32) // R
    coarse = jnp.arange(TA, dtype=jnp.int32)
    return jnp.where(coarse[:, None] == block_of[None, :], 1.0 / R, 0.0).astype(jnp.float32)


def fire_tile(level, fuel, base, wind, average):
    heat = jnp.zeros_like(fuel)
    for substep in range(KSUB):
        padded = jnp.pad(level, 1, mode="edge")
        grad_x = 0.5 * (padded[2:, 1:-1] - padded[:-2, 1:-1])
        grad_y = 0.5 * (padded[1:-1, 2:] - padded[1:-1, :-2])
        laplace = (
            padded[2:, 1:-1]
            + padded[:-2, 1:-1]
            + padded[1:-1, 2:]
            + padded[1:-1, :-2]
            - 4.0 * level
        )
        length = jnp.sqrt(grad_x * grad_x + grad_y * grad_y + regular)
        along = (wind[0] * grad_x + wind[1] * grad_y) / length
        speed = base * jnp.maximum(1.0 + along, 0.0)
        level = level - time_step * speed * length + diffusion * laplace
        used = burn_rate * fuel * jax.nn.sigmoid(-sharpness * level)
        fuel = fuel - used
        heat = heat + used
    flux = jnp.dot(
        jnp.dot(average, heat, precision=lax.Precision.HIGHEST),
        average.T,
        precision=lax.Precision.HIGHEST,
    )
    return (level, fuel, flux)


def body(theta, wind_u, wind_v, level_set, fuel_load, spread_base, tile_owner, tile_place):
    cycle = lax.axis_size("gx")
    cells_x = theta.shape[1]
    cells_y = theta.shape[2]
    tiles_y = cells_y // TA
    interp = interp_table()
    average = average_table()
    owners = tile_owner[0, 0]
    places = tile_place[0, 0]
    same_owner = owners[:, None] == owners[None, :]
    earlier = jnp.arange(TPD)[None, :] < jnp.arange(TPD)[:, None]
    slot_rank = jnp.sum(jnp.logical_and(same_owner, earlier), axis=1)
    slot_index = owners * CAP + slot_rank
    request = jnp.full((cycle * CAP,), -1, jnp.int32).at[slot_index].set(places).reshape(cycle, CAP)
    asked = lax.all_to_all(request, "gx", split_axis=0, concat_axis=0, tiled=True).reshape(
        cycle * CAP
    )
    surface = jnp.stack([wind_u[0], wind_v[0]])
    rimmed = padded_2(surface, (("gx", 1), ("gy", 2)), 1)
    valid = asked >= 0
    safe_place = jnp.maximum(asked, 0)
    start_x = safe_place // tiles_y * TA
    start_y = safe_place % tiles_y * TA

    def cut(left, bottom):
        return lax.dynamic_slice(rimmed, (jnp.int32(0), left, bottom), (2, TA + 2, TA + 2))

    patches = jax.vmap(cut)(start_x, start_y)
    fine_wind = jnp.einsum(
        "ak,tckl,bl->tcab", interp, patches, interp, precision=lax.Precision.HIGHEST
    )
    returned = lax.all_to_all(
        fine_wind.reshape(cycle, CAP, 2, S, S), "gx", split_axis=0, concat_axis=0, tiled=True
    )
    tile_wind = returned.reshape(cycle * CAP, 2, S, S)[slot_index]
    level_out, fuel_out, fluxes = jax.vmap(lambda a, b, c, d: fire_tile(a, b, c, d, average))(
        level_set[0, 0], fuel_load[0, 0], spread_base[0, 0], tile_wind
    )
    outbox = (
        jnp.zeros((cycle * CAP, TA * TA), jnp.float32)
        .at[slot_index]
        .set(fluxes.reshape(TPD, TA * TA))
        .reshape(cycle, CAP, TA * TA)
    )
    padded = padded_2(theta, (("gx", 1), ("gy", 2)), 1)
    advect = courant * (
        jnp.maximum(wind_u, 0.0) * (theta - padded[:, :-2, 1:-1])
        + jnp.minimum(wind_u, 0.0) * (padded[:, 2:, 1:-1] - theta)
        + jnp.maximum(wind_v, 0.0) * (theta - padded[:, 1:-1, :-2])
        + jnp.minimum(wind_v, 0.0) * (padded[:, 1:-1, 2:] - theta)
    )
    inbox = lax.all_to_all(outbox, "gx", split_axis=0, concat_axis=0, tiled=True).reshape(
        cycle * CAP, TA, TA
    )
    offsets = jnp.arange(TA, dtype=jnp.int32)
    row_start = jnp.where(valid, start_x, cells_x + TA)
    index_x = jnp.broadcast_to(
        row_start[:, None, None] + offsets[None, :, None], (cycle * CAP, TA, TA)
    )
    index_y = jnp.broadcast_to(
        start_y[:, None, None] + offsets[None, None, :], (cycle * CAP, TA, TA)
    )
    field = jnp.zeros((cells_x, cells_y), jnp.float32).at[index_x, index_y].add(inbox, mode="drop")
    profile = jnp.exp(-(jnp.arange(LZ, dtype=jnp.float32) + 0.5) / (LZ / 4.0))
    theta_next = theta - advect + heat_gain * field[None, :, :] * profile[:, None, None]
    return (theta_next, level_out[None, None], fuel_out[None, None])


def solution(mesh):
    in_specs = (
        P(None, "gx", "gy"),
        P(None, "gx", "gy"),
        P(None, "gx", "gy"),
        P("gx", "gy", None, None, None),
        P("gx", "gy", None, None, None),
        P("gx", "gy", None, None, None),
        P("gx", "gy", None),
        P("gx", "gy", None),
    )
    out_specs = (
        P(None, "gx", "gy"),
        P("gx", "gy", None, None, None),
        P("gx", "gy", None, None, None),
    )
    return jax.shard_map(body, mesh=mesh, in_specs=in_specs, out_specs=out_specs, check_vma=False)
```

profile of v0, /device:TPU:0, one launch (start us, length us, event | category | flops | bytes accessed | tf_op | source)
XLA Modules:
  0.0 195.8 jit_solution(8774067842660667991)
XLA Ops:
  2.2 4.8 %collective-permute-start.4 = (f32[2,1,128]{2,0,1:T(2,128)S(1)}, f32[2,1,128]{2,0,1:T(2,128)S(1)}, u32[]{:S(2)}, u32[]{:S(2)}) collective-permute-start(f32[2,1,128]{2,0,1:T(2,128)S(1)} %get-tuple-element.63), channel_id=1, source_target_pairs={{0,4},{4,8},{8,12},{12,16},{16,20},{20,24},{24,28},{1,5},{5,9},{9,... | collective-permute-start | bytes 3080 | tf_op jit(solution)/shard_map/ppermute | solution.py:32
  7.0 1.3 collective-permute-start.5
  11.3 7.0 %all-to-all-start = ((s32[8,1,2]{2,1,0:T(1,128)}), s32[8,1,2]{2,1,0:T(1,128)S(1)}, u32[]{:S(2)}, u32[]{:S(2)}) async-start(s32[8,1,2]{2,1,0:T(1,128)} %bitcast.5), calls=%async_computation | async-start | bytes 8192 | tf_op jit(solution)/shard_map/all_to_all | solution.py:95
  18.3 6.4 %all-to-all-done = s32[8,1,2]{2,1,0:T(1,128)S(1)} async-done(((s32[8,1,2]{2,1,0:T(1,128)}), s32[8,1,2]{2,1,0:T(1,128)S(1)}, u32[]{:S(2)}, u32[]{:S(2)}) %all-to-all-start) | async-done | bytes 96 | tf_op jit(solution)/shard_map/all_to_all | solution.py:95
  25.2 1.3 collective-permute-start.6
  26.5 1.3 collective-permute-start.7
  27.9 3.6 %collective-permute-done.7 = f32[2,66,1]{2,0,1:T(2,128)S(1)} collective-permute-done((f32[2,66,1]{2,0,1:T(2,128)S(1)}, f32[2,66,1]{2,0,1:T(2,128)S(1)}, u32[]{:S(2)}, u32[]{:S(2)}) %collective-permute-start.7) | collective-permute-done | bytes 560 | tf_op jit(solution)/shard_map/ppermute | solution.py:34
  31.9 31.6 %while.1 = (s32[]{:T(128)}, f32[2,66,130]{2,0,1:T(2,128)S(1)}, s32[16,3]{0,1:T(4,128)S(1)}, f32[16,2,6,6]{3,1,2,0:T(2,128)S(1)}, s32[]{:T(128)}) while((s32[]{:T(128)}, f32[2,66,130]{2,0,1:T(2,128)S(1)}, s32[16,3]{0,1:T(4,128)S(1)}, f32[16,2,6,6]{3,1,2,0:T(2,128)S(1)}, s32[]{:T(128)}) %tuple.54), condition=%wide.while_cond, body=%wide.while_body.sunk | while | flops 2 | bytes 12405 | solution.py:106
  32.5 1.4 bitcast_dynamic-update-slice_fusion.2
  34.5 1.4 bitcast_dynamic-update-slice_fusion.2
  36.4 1.4 bitcast_dynamic-update-slice_fusion.2
  38.4 1.4 bitcast_dynamic-update-slice_fusion.2
  40.4 1.4 bitcast_dynamic-update-slice_fusion.2
  42.4 1.4 bitcast_dynamic-update-slice_fusion.2
  44.3 1.4 bitcast_dynamic-update-slice_fusion.2
  46.3 1.4 bitcast_dynamic-update-slice_fusion.2
  48.3 1.4 bitcast_dynamic-update-slice_fusion.2
  50.3 1.4 bitcast_dynamic-update-slice_fusion.2
  52.2 1.4 bitcast_dynamic-update-slice_fusion.2
  54.2 1.4 bitcast_dynamic-update-slice_fusion.2
  56.2 1.4 bitcast_dynamic-update-slice_fusion.2
  58.2 1.4 bitcast_dynamic-update-slice_fusion.2
  60.1 1.4 bitcast_dynamic-update-slice_fusion.2
  62.1 1.4 bitcast_dynamic-update-slice_fusion.2
  64.1 4.8 %fusion.49 = f32[16,2,128,128]{3,2,1,0:T(8,128)} fusion(f32[16,2,6,128]{3,0,2,1:T(8,128)S(1)} %fusion.62, f32[128]{0:T(128)S(1)} %multiply_add_fusion), kind=kOutput, calls=%fused_computation.134 | convolution fusion | flops 37751808 | bytes 2195968 | tf_op jit(solution)/shard_map/ak,tckl,bl->tcab/dot_general | solution.py:109
  68.8 4.6 %all-to-all-start.1 = ((f32[8,2,2,128,128]{4,3,2,1,0:T(8,128)}), f32[8,2,2,128,128]{4,3,2,1,0:T(8,128)}, u32[]{:S(2)}, u32[]{:S(2)}) async-start(f32[8,2,2,128,128]{4,3,2,1,0:T(8,128)} %bitcast.162), calls=%async_computation.1 | async-start | bytes 4194304 | tf_op jit(solution)/shard_map/all_to_all | solution.py:112
  73.5 3.8 %collective-permute-start = (f32[80,1,128]{2,1,0:T(1,128)S(1)}, f32[80,1,128]{2,1,0:T(1,128)S(1)}, u32[]{:S(2)}, u32[]{:S(2)}) collective-permute-start(f32[80,1,128]{2,1,0:T(1,128)S(1)} %get-tuple-element.35), channel_id=1, source_target_pairs={{0,4},{4,8},{8,12},{12,16},{16,20},{20,24},{24,28},{1,5},{5,9},{9,... | collective-permute-start | bytes 122888 | tf_op jit(solution)/shard_map/ppermute | solution.py:32
  79.5 1.3 pad_maximum_fusion.9
  80.9 1.8 fusion.110
  83.1 6.7 %collective-permute-done = f32[80,1,128]{2,1,0:T(1,128)S(1)} collective-permute-done((f32[80,1,128]{2,1,0:T(1,128)S(1)}, f32[80,1,128]{2,1,0:T(1,128)S(1)}, u32[]{:S(2)}, u32[]{:S(2)}) %collective-permute-start) | collective-permute-done | bytes 40992 | tf_op jit(solution)/shard_map/ppermute | solution.py:32
  90.3 2.5 %fusion.103 = (f32[80,66,1]{2,1,0:T(8,128)}, f32[80,66,1]{2,1,0:T(8,128)S(1)}) fusion(f32[80,66,128]{2,1,0:T(8,128)S(1)} %pad_maximum_fusion), kind=kLoop, calls=%fused_computation.222 | loop fusion | bytes 84480 | tf_op jit(solution)/shard_map/slice | solution.py:29
  92.8 2.7 %copy.65 = f32[80,66,1]{0,1,2:T(8,128)S(1)} copy(f32[80,66,1]{2,1,0:T(8,128)} %get-tuple-element.33) | data formatting | bytes 42240 | tf_op jit(solution)/shard_map/slice | solution.py:29
  95.5 5.6 %collective-permute-start.2 = (f32[80,66,1]{0,1,2:T(8,128)S(1)}, f32[80,66,1]{0,1,2:T(8,128)S(1)}, u32[]{:S(2)}, u32[]{:S(2)}) collective-permute-start(f32[80,66,1]{0,1,2:T(8,128)S(1)} %copy.65), channel_id=1, source_target_pairs={{0,1},{1,2},{2,3},{4,5},{5,6},{6,7},{8,9},{9,10},{10,11},{12,13},{... | collective-permute-start | bytes 63368 | tf_op jit(solution)/shard_map/ppermute | solution.py:32
  102.1 1.5 collective-permute-start.3
  103.6 17.9 %all-to-all-done.1 = f32[8,2,2,128,128]{4,3,2,1,0:T(8,128)} async-done(((f32[8,2,2,128,128]{4,3,2,1,0:T(8,128)}), f32[8,2,2,128,128]{4,3,2,1,0:T(8,128)}, u32[]{:S(2)}, u32[]{:S(2)}) %all-to-all-start.1) | async-done | bytes 2097184 | tf_op jit(solution)/shard_map/all_to_all | solution.py:112
  121.5 2.4 %gather_fusion = f32[16,2,128,128]{3,2,1,0:T(8,128)S(1)} fusion(f32[16,2,128,128]{3,2,1,0:T(8,128)} %bitcast.15, s32[1024]{0:T(1024)S(1)} %pad_clamp_fusion), kind=kCustom, calls=%fused_computation | custom fusion | bytes 4194368 | tf_op jit(solution)/shard_map/gather | solution.py:115
  123.8 5.2 %fusion.17 = f32[16,128,128]{2,1,0:T(8,128)S(1)} fusion(f32[16,128,128]{2,1,0:T(8,128)} %bitcast.165, f32[1,1,16,128,128]{4,3,2,1,0:T(8,128)S(1)} %copy-done, f32[16,130,1]{2,1,0:T(8,128)} %get-tuple-element.48, f32[16,1,128]{2,1,0:T(1,128)S(1)} %get-tuple-element.60, f32[16,1,128]{2,1,0:T(1,128)S(1)} %get-tuple-element.59, ...), kind=kLoop, calls=%fused_computation.94 | loop fusion | flops 8650752 | bytes 5275904 | tf_op jit(solution)/shard_map/vmap()/add | solution.py:69
  129.5 2.2 %fusion.21 = f32[16,128,128]{2,1,0:T(8,128)S(1)} fusion(f32[16,128,128]{2,1,0:T(8,128)S(1)} %fusion.17, f32[1,1,16,128,128]{4,3,2,1,0:T(8,128)S(1)} %copy-done, f32[16,130,1]{2,1,0:T(8,128)S(1)} %get-tuple-element.46, f32[16,1,128]{2,1,0:T(1,128)S(1)} %get-tuple-element.58, f32[16,1,128]{2,1,0:T(1,128)S(1)} %get-tuple-element.57, ...), kind=kLoop, calls=%fused_computation.98 | loop fusion | flops 8650752 | bytes 5275904 | tf_op jit(solution)/shard_map/vmap()/add | solution.py:69
  132.2 2.2 %fusion.25 = f32[16,128,128]{2,1,0:T(8,128)S(1)} fusion(f32[16,128,128]{2,1,0:T(8,128)S(1)} %fusion.21, f32[1,1,16,128,128]{4,3,2,1,0:T(8,128)S(1)} %copy-done, f32[16,130,1]{2,1,0:T(8,128)S(1)} %get-tuple-element.44, f32[16,1,128]{2,1,0:T(1,128)S(1)} %get-tuple-element.56, f32[16,1,128]{2,1,0:T(1,128)S(1)} %get-tuple-element.55, ...), kind=kLoop, calls=%fused_computation.102 | loop fusion | flops 8650752 | bytes 5275904 | tf_op jit(solution)/shard_map/vmap()/add | solution.py:69
  134.9 2.2 %fusion.29 = f32[16,128,128]{2,1,0:T(8,128)S(1)} fusion(f32[16,128,128]{2,1,0:T(8,128)S(1)} %fusion.25, f32[1,1,16,128,128]{4,3,2,1,0:T(8,128)S(1)} %copy-done, f32[16,130,1]{2,1,0:T(8,128)S(1)} %get-tuple-element.42, f32[16,1,128]{2,1,0:T(1,128)S(1)} %get-tuple-element.54, f32[16,1,128]{2,1,0:T(1,128)S(1)} %get-tuple-element.53, ...), kind=kLoop, calls=%fused_computation.106 | loop fusion | flops 8650752 | bytes 5275904 | tf_op jit(solution)/shard_map/vmap()/add | solution.py:69
  137.6 2.2 %fusion.33 = f32[16,128,128]{2,1,0:T(8,128)S(1)} fusion(f32[16,128,128]{2,1,0:T(8,128)S(1)} %fusion.29, f32[1,1,16,128,128]{4,3,2,1,0:T(8,128)S(1)} %copy-done, f32[16,130,1]{2,1,0:T(8,128)S(1)} %get-tuple-element.40, f32[16,1,128]{2,1,0:T(1,128)S(1)} %get-tuple-element.52, f32[16,1,128]{2,1,0:T(1,128)S(1)} %get-tuple-element.51, ...), kind=kLoop, calls=%fused_computation.110 | loop fusion | flops 8650752 | bytes 5275904 | tf_op jit(solution)/shard_map/vmap()/add | solution.py:69
  141.1 4.5 %subtract_bitcast_fusion = (f32[1,1,16,128,128]{4,3,2,1,0:T(8,128)}, f32[16,128,128]{2,1,0:T(8,128)S(1)}) fusion(f32[16,128,128]{2,1,0:T(8,128)S(1)} %fusion.33, f32[16,128,128]{2,1,0:T(8,128)S(1)} %fusion.29, f32[16,128,128]{2,1,0:T(8,128)S(1)} %fusion.25, f32[16,128,128]{2,1,0:T(8,128)S(1)} %fusion.21, f32[16,128,128]{2,1,0:T(8,128)S(1)} %fusion.17, ...), kind=kLoop, calls=%fused_computation.118 | loop fusion | flops 19660800 | bytes 11567360 | tf_op jit(solution)/shard_map/broadcast_in_dim | solution.py:146
  145.6 2.5 %fusion.39 = f32[4,16,128]{2,0,1:T(4,128)S(1)} fusion(f32[16,128,128]{2,1,0:T(8,128)S(1)} %fusion.21, f32[1,1,16,128,128]{4,3,2,1,0:T(8,128)S(1)} %copy-done.2, f32[16,128,128]{2,1,0:T(8,128)S(1)} %fusion.17, f32[16,128,128]{2,1,0:T(8,128)S(1)} %get-tuple-element.30, f32[16,128,128]{2,1,0:T(8,128)S(1)} %fusion.33, f32[16,128,128]{2,1,0:T(8,128)S(1)} %fusion.29, ...), kind=kOutput, calls=%fused_computation.119 | convolution fusion | flops 24642560 | bytes 7373312 | tf_op jit(solution)/shard_map/vmap()/dot_general | solution.py:74
  149.7 15.4 %all-to-all-start.2 = ((f32[8,2,16]{2,1,0:T(2,128)}), f32[8,2,16]{2,1,0:T(2,128)S(1)}, u32[]{:S(2)}, u32[]{:S(2)}) async-start(f32[8,2,16]{2,1,0:T(2,128)} %bitcast.20), calls=%async_computation.2 | async-start | bytes 16384 | tf_op jit(solution)/shard_map/all_to_all | solution.py:132
  166.4 2.5 %copy.68 = f32[80,66,1]{2,1,0:T(8,128)} copy(f32[80,66,1]{0,1,2:T(8,128)S(1)} %collective-permute-done.3) | data formatting | bytes 42240 | tf_op jit(solution)/shard_map/ppermute | solution.py:34
  168.9 2.7 %all-to-all-done.2 = f32[8,2,16]{2,1,0:T(2,128)S(1)} async-done(((f32[8,2,16]{2,1,0:T(2,128)}), f32[8,2,16]{2,1,0:T(2,128)S(1)}, u32[]{:S(2)}, u32[]{:S(2)}) %all-to-all-start.2) | async-done | bytes 1056 | tf_op jit(solution)/shard_map/all_to_all | solution.py:132
  171.7 12.8 %scatter_fusion = f32[64,128]{1,0:T(8,128)S(1)} fusion(f32[64,128]{1,0:T(8,128)S(1)} %broadcast_in_dim.32, s32[256]{0:T(256)S(1)} %reshape.317, f32[256]{0:T(256)S(1)} %reshape.319), kind=kCustom, calls=%fused_computation.3 | custom fusion | flops 256 | bytes 5120 | tf_op jit(solution)/shard_map/scatter-add | solution.py:143
  184.6 11.3 %fusion.5 = f32[80,64,128]{2,1,0:T(8,128)} fusion(f32[80,64,128]{2,1,0:T(8,128)} %param.8, f32[80,66,1]{2,1,0:T(8,128)} %copy.68, f32[80,1,128]{2,1,0:T(1,128)S(1)} %collective-permute-done.1, f32[80,1,128]{2,1,0:T(1,128)S(1)} %collective-permute-done, f32[80,66,1]{2,1,0:T(8,128)S(1)} %copy.66, f32[80,64,128]{2,1,0:T(8,128)} %param.10, ...), kind=kLoop, calls=%fused_computation.13 | loop fusion | flops 17694720 | bytes 10643008 | tf_op jit(solution)/shard_map/add | solution.py:145
  (107 shorter events, 25.9 us)
Async XLA Ops:
  2.2 22.9 %collective-permute-start.4 = (f32[2,1,128]{2,0,1:T(2,128)S(1)}, f32[2,1,128]{2,0,1:T(2,128)S(1)}, u32[]{:S(2)}, u32[]{:S(2)}) collective-permute-start(f32[2,1,128]{2,0,1:T(2,128)S(1)} %get-tuple-element.63), channel_id=1, source_target_pairs={{0,4},{4,8},{8,12},{12,16},{16,20},{20,24},{24,28},{1,5},{5,9},{9,... | collective-permute-start | bytes 3080 | tf_op jit(solution)/shard_map/ppermute | solution.py:32
  7.0 18.0 %collective-permute-start.5 = (f32[2,1,128]{2,0,1:T(2,128)S(1)}, f32[2,1,128]{2,0,1:T(2,128)S(1)}, u32[]{:S(2)}, u32[]{:S(2)}) collective-permute-start(f32[2,1,128]{2,0,1:T(2,128)S(1)} %get-tuple-element.64), channel_id=1, source_target_pairs={{4,0},{8,4},{12,8},{16,12},{20,16},{24,20},{28,24},{5,1},{9,5},{13... | collective-permute-start | bytes 3080 | tf_op jit(solution)/shard_map/ppermute | solution.py:34
  11.3 13.3 %all-to-all-start = ((s32[8,1,2]{2,1,0:T(1,128)}), s32[8,1,2]{2,1,0:T(1,128)S(1)}, u32[]{:S(2)}, u32[]{:S(2)}) async-start(s32[8,1,2]{2,1,0:T(1,128)} %bitcast.5), calls=%async_computation | async-start | bytes 8192 | tf_op jit(solution)/shard_map/all_to_all | solution.py:95
  25.2 2.6 %collective-permute-start.6 = (f32[2,66,1]{2,0,1:T(2,128)S(1)}, f32[2,66,1]{2,0,1:T(2,128)S(1)}, u32[]{:S(2)}, u32[]{:S(2)}) collective-permute-start(f32[2,66,1]{2,0,1:T(2,128)S(1)} %get-tuple-element.61), channel_id=1, source_target_pairs={{0,1},{1,2},{2,3},{4,5},{5,6},{6,7},{8,9},{9,10},{10,11},{12,13},{... | collective-permute-start | bytes 1592 | tf_op jit(solution)/shard_map/ppermute | solution.py:32
  26.5 4.9 %collective-permute-start.7 = (f32[2,66,1]{2,0,1:T(2,128)S(1)}, f32[2,66,1]{2,0,1:T(2,128)S(1)}, u32[]{:S(2)}, u32[]{:S(2)}) collective-permute-start(f32[2,66,1]{2,0,1:T(2,128)S(1)} %get-tuple-element.62), channel_id=1, source_target_pairs={{1,0},{2,1},{3,2},{5,4},{6,5},{7,6},{9,8},{10,9},{11,10},{13,12},{... | collective-permute-start | bytes 1592 | tf_op jit(solution)/shard_map/ppermute | solution.py:34
  68.8 4.6 %copy-start.1 = (f32[80,64,128]{2,1,0:T(8,128)S(1)}, f32[80,64,128]{2,1,0:T(8,128)}, u32[]{:S(2)}) copy-start(f32[80,64,128]{2,1,0:T(8,128)} %param.8) | copy-start | bytes 7864324
  68.8 52.6 %all-to-all-start.1 = ((f32[8,2,2,128,128]{4,3,2,1,0:T(8,128)}), f32[8,2,2,128,128]{4,3,2,1,0:T(8,128)}, u32[]{:S(2)}, u32[]{:S(2)}) async-start(f32[8,2,2,128,128]{4,3,2,1,0:T(8,128)} %bitcast.162), calls=%async_computation.1 | async-start | bytes 4194304 | tf_op jit(solution)/shard_map/all_to_all | solution.py:112
  73.5 16.3 %collective-permute-start = (f32[80,1,128]{2,1,0:T(1,128)S(1)}, f32[80,1,128]{2,1,0:T(1,128)S(1)}, u32[]{:S(2)}, u32[]{:S(2)}) collective-permute-start(f32[80,1,128]{2,1,0:T(1,128)S(1)} %get-tuple-element.35), channel_id=1, source_target_pairs={{0,4},{4,8},{8,12},{12,16},{16,20},{20,24},{24,28},{1,5},{5,9},{9,... | collective-permute-start | bytes 122888 | tf_op jit(solution)/shard_map/ppermute | solution.py:32
  77.3 12.5 %collective-permute-start.1 = (f32[80,1,128]{2,1,0:T(1,128)S(1)}, f32[80,1,128]{2,1,0:T(1,128)S(1)}, u32[]{:S(2)}, u32[]{:S(2)}) collective-permute-start(f32[80,1,128]{2,1,0:T(1,128)S(1)} %get-tuple-element.36), channel_id=1, source_target_pairs={{4,0},{8,4},{12,8},{16,12},{20,16},{24,20},{28,24},{5,1},{9,5},{13... | collective-permute-start | bytes 122888 | tf_op jit(solution)/shard_map/ppermute | solution.py:34
  95.5 69.8 %collective-permute-start.2 = (f32[80,66,1]{0,1,2:T(8,128)S(1)}, f32[80,66,1]{0,1,2:T(8,128)S(1)}, u32[]{:S(2)}, u32[]{:S(2)}) collective-permute-start(f32[80,66,1]{0,1,2:T(8,128)S(1)} %copy.65), channel_id=1, source_target_pairs={{0,1},{1,2},{2,3},{4,5},{5,6},{6,7},{8,9},{9,10},{10,11},{12,13},{... | collective-permute-start | bytes 63368 | tf_op jit(solution)/shard_map/ppermute | solution.py:32
  102.1 64.4 %collective-permute-start.3 = (f32[80,66,1]{0,1,2:T(8,128)S(1)}, f32[80,66,1]{0,1,2:T(8,128)S(1)}, u32[]{:S(2)}, u32[]{:S(2)}) collective-permute-start(f32[80,66,1]{0,1,2:T(8,128)S(1)} %copy.67), channel_id=1, source_target_pairs={{1,0},{2,1},{3,2},{5,4},{6,5},{7,6},{9,8},{10,9},{11,10},{13,12},{... | collective-permute-start | bytes 63368 | tf_op jit(solution)/shard_map/ppermute | solution.py:34
  121.5 2.4 %copy-start = (f32[1,1,16,128,128]{4,3,2,1,0:T(8,128)S(1)}, f32[1,1,16,128,128]{4,3,2,1,0:T(8,128)}, u32[]{:S(2)}) copy-start(f32[1,1,16,128,128]{4,3,2,1,0:T(8,128)} %param.13) | copy-start | bytes 3145732
  139.9 1.2 copy-start.2
  145.6 2.5 %copy-start.3 = (f32[16,128,128]{2,1,0:T(8,128)}, f32[16,128,128]{2,1,0:T(8,128)S(1)}, u32[]{:S(2)}) copy-start(f32[16,128,128]{2,1,0:T(8,128)S(1)} %get-tuple-element.30) | copy-start | bytes 3145732
  149.7 21.9 %all-to-all-start.2 = ((f32[8,2,16]{2,1,0:T(2,128)}), f32[8,2,16]{2,1,0:T(2,128)S(1)}, u32[]{:S(2)}, u32[]{:S(2)}) async-start(f32[8,2,16]{2,1,0:T(2,128)} %bitcast.20), calls=%async_computation.2 | async-start | bytes 16384 | tf_op jit(solution)/shard_map/all_to_all | solution.py:132
where the time goes:
time: 197 us; the launch traced here: 196 us
  local copies, waits for them, and re-layouts  54.4 us (28%)
  starting transfers between devices  47.9 us (24%)
  other arithmetic  47.2 us (24%)
  waiting for transfers between devices  37.2 us (19%)
  matrix products  7.96 us (4%)
    gather x48, local copies, waits for them, and re-layouts  31.6 us
    all_to_all x1, waiting for transfers between devices, body(): lax.all_to_all(fine_wind.reshape(cycle, CAP, 2, S, S), 'gx', split_axis=0...  17.9 us
    ppermute x4, starting transfers between devices, padded_2(): lax.ppermute(tail, axis, [(i, (i + 1) % count) for i in range(ends)])  15.5 us
    all_to_all x1, starting transfers between devices, body(): lax.all_to_all(outbox, 'gx', split_axis=0, concat_axis=0, tiled=True)  15.4 us
    add x5, other arithmetic, fire_tile(): level = level - time_step * speed * length + diffusion * laplace  13.9 us
    scatter-add x1, other arithmetic, body(): jnp.zeros((cells_x, cells_y), jnp.float32).at[index_x, index_y]  12.8 us
    add x1, other arithmetic, body(): theta - advect + heat_gain * field[None, :, :] * profile[:, None, None]  11.3 us
    all_to_all x1, starting transfers between devices, body(): lax.all_to_all(request, 'gx', split_axis=0, concat_axis=0, tiled=True)  6.96 us
  transfers between devices with their start and end apart: 11, of which 5 were waited for; matrix products, arithmetic and copies ran while one was open for 23% of the time, Pallas kernels for 0%

commit v1 on v0

v1 whole, which is shorter than its diff:
```python
import functools

import jax
import jax.numpy as jnp
from jax import lax
from jax.experimental import pallas as pl
from jax.experimental.pallas import tpu as pltpu
from jax.sharding import PartitionSpec as P

TA = 4
R = 32
KSUB = 6
CAP = 2
TPD = 16
S = 128
BX = 64
BY = 128
GROUP = 8

MESH = pl.DeviceIdType.MESH
F32 = jnp.float32
BF16 = jnp.bfloat16


def iota(shape, dim):
    return lax.broadcasted_iota(jnp.int32, shape, dim)


def pieces(x):
    high = x.astype(BF16)
    rest = x - high.astype(F32)
    middle = rest.astype(BF16)
    low = (rest - middle.astype(F32)).astype(BF16)
    return (high, middle, low)


def dot(a, b):
    return jnp.dot(a, b, preferred_element_type=F32)


def dot_left_exact(a, b):
    a = a.astype(BF16)
    high, middle, low = pieces(b)
    return dot(a, high) + (dot(a, middle) + dot(a, low))


def dot_right_exact(a, b):
    b = b.astype(BF16)
    high, middle, low = pieces(a)
    return dot(high, b) + (dot(middle, b) + dot(low, b))


def interp_weight(fine, column):
    where_fine = (fine.astype(F32) + 0.5) / R + 0.5
    return jnp.maximum(0.0, 1.0 - jnp.abs(where_fine - column.astype(F32)))


def kernel(
    G, H, LZ,
    theta_hbm, u_hbm, v_hbm, level_hbm, fuel_hbm, base_hbm, owner_ref, place_ref,
    part_hbm, level_out, fuel_out, field_ref,
    th, uu, vv, part, lev, spare, fin, fout, base, wind, wide, small, rows, code_col,
    req_out, req_in, rep_out, rep_in, flux_out, flux_in,
    yw_out, yw_in, yth_out, yth_in, xth_out, xth_in,
    in_sem, lev_sem, fuel_sem, part_sem,
    req_send, req_recv, rep_send, rep_recv, flux_send, flux_recv,
    yw_send, yw_recv, th_send, th_recv,
):
    Q = G * CAP
    i = lax.axis_index("gx")
    j = lax.axis_index("gy")

    def gx(offset):
        return lax.rem(i + (offset % G), G)

    def gy(offset):
        return lax.rem(j + (offset % H), H)

    loads = [
        pltpu.make_async_copy(u_hbm.at[0], uu.at[0], in_sem.at[0]),
        pltpu.make_async_copy(v_hbm.at[0], vv.at[0], in_sem.at[1]),
        pltpu.make_async_copy(theta_hbm, th.at[:, 8:8 + BX, :], in_sem.at[2]),
        pltpu.make_async_copy(u_hbm.at[1:], uu.at[1:], in_sem.at[3]),
        pltpu.make_async_copy(v_hbm.at[1:], vv.at[1:], in_sem.at[4]),
        pltpu.make_async_copy(level_hbm.at[0, 0], lev.at[:, 8:8 + S, :], in_sem.at[5]),
        pltpu.make_async_copy(fuel_hbm.at[0, 0], fin, in_sem.at[6]),
        pltpu.make_async_copy(base_hbm.at[0, 0], base, in_sem.at[7]),
    ]
    for load in loads:
        load.start()

    corners = [(0, 1), (0, -1), (-1, 1), (-1, -1), (1, 1), (1, -1)]
    barrier = pltpu.get_barrier_semaphore()
    for o in range(1, G):
        pl.semaphore_signal(barrier, inc=1, device_id=(gx(o), j), device_id_type=MESH)
    for dx, dy in corners:
        pl.semaphore_signal(barrier, inc=1, device_id=(gx(dx), gy(dy)), device_id_type=MESH)

    lane = iota((8, 128), 1)
    lane16 = lane & (TPD - 1)
    sub16 = iota((TPD, 128), 0)
    own_row = jnp.zeros((8, 128), jnp.int32)
    place_row = jnp.zeros((8, 128), jnp.int32)
    own_col = jnp.zeros((TPD, 128), jnp.int32)
    for t in range(TPD):
        own_row = jnp.where(lane16 == t, owner_ref[0, 0, t], own_row)
        place_row = jnp.where(lane16 == t, place_ref[0, 0, t], place_row)
        own_col = jnp.where(sub16 == t, owner_ref[0, 0, t], own_col)
    rank_row = jnp.zeros((8, 128), jnp.int32)
    rank_col = jnp.zeros((TPD, 128), jnp.int32)
    for t in range(TPD):
        rank_row += jnp.where(
            jnp.logical_and(own_row == owner_ref[0, 0, t], lane16 > t), 1, 0)
        rank_col += jnp.where(
            jnp.logical_and(own_col == owner_ref[0, 0, t], sub16 > t), 1, 0)

    def code_of(owner, rank):
        away = owner - i
        return jnp.where(away < 0, away + G, away) * CAP + rank

    code_row = code_of(own_row, rank_row)
    code_col[...] = code_of(own_col, rank_col)

    row1 = code_row[0:1]
    place1 = place_row[0:1]
    wanted = jnp.where(
        jnp.logical_and(row1 == iota((Q, 128), 0), iota((Q, 128), 1) < TPD),
        place1 + 1, 0).astype(F32)
    asked = jnp.broadcast_to(jnp.sum(wanted, axis=1, keepdims=True) - 1.0, (Q, 128))

    loads[0].wait()
    loads[1].wait()
    for o in range(G):
        req_out[o, 0:2, :] = asked[2 * o:2 * o + 2]
        edge = 0 if o == G - 1 else BX - 1
        req_out[o, 2:3, :] = uu[0, edge:edge + 1, :]
        req_out[o, 3:4, :] = vv[0, edge:edge + 1, :]
    packed = jnp.zeros((8, 128), F32)
    for g in range(16):
        source = uu if g < 8 else vv
        cell = source[0, 8 * (g % 8):8 * (g % 8) + 8, :]
        packed = jnp.where((lane >> 1) == g, pltpu.roll(cell, 2 * g + 1, 1), packed)
    yw_out[...] = packed

    pl.semaphore_wait(barrier, G - 1 + len(corners))

    def to_peer(o, out, into, send, recv):
        return pltpu.make_async_remote_copy(
            src_ref=out, dst_ref=into, send_sem=send, recv_sem=recv,
            device_id=(gx(o), j), device_id_type=MESH)

    requests = [
        to_peer(o, req_out.at[o], req_in.at[o], req_send.at[o], req_recv.at[o])
        for o in range(1, G)
    ]
    winds = [
        pltpu.make_async_remote_copy(
            src_ref=yw_out, dst_ref=yw_in.at[n], send_sem=yw_send.at[n],
            recv_sem=yw_recv.at[n], device_id=(gx(dx), gy(dy)), device_id_type=MESH)
        for n, (dx, dy) in enumerate(corners)
    ]
    for copy in requests + winds:
        copy.start()
    req_in[0] = req_out[0]

    fine_of = iota((2 * S, 48), 0)
    slot_of = iota((2 * S, 48), 1) & 15
    column = slot_of - 6 * (fine_of >> 7)
    a3 = jnp.where(
        jnp.logical_and(column >= 0, column < 6),
        interp_weight(fine_of & (S - 1), column), 0.0).astype(BF16)
    wide[...] = a3

    loads[2].wait()

    def pack(zz, carry):
        acc = jnp.zeros((8, 128), F32)
        for zl in range(GROUP):
            z = zz * GROUP + zl
            for g in range(8):
                n = zl * 8 + g
                cell = th[z, 8 + 8 * g:16 + 8 * g, :]
                acc = jnp.where((lane >> 1) == n, pltpu.roll(cell, (2 * n + 1) % 128, 1), acc)
            xth_out[0, pl.ds(z, 1), :] = th[z, 7 + BX:8 + BX, :]
            xth_out[1, pl.ds(z, 1), :] = th[z, 8:9, :]
        yth_out[pl.ds(pl.multiple_of(zz * 8, 8), 8), :] = acc
        return carry

    lax.fori_loop(0, LZ // GROUP, pack, 0)
    halos = []
    for n, (out, into, dx, dy) in enumerate([
        (xth_out.at[0], xth_in.at[0], 1, 0),
        (xth_out.at[1], xth_in.at[1], -1, 0),
        (yth_out, yth_in.at[0], 0, 1),
        (yth_out, yth_in.at[1], 0, -1),
    ]):
        halos.append(pltpu.make_async_remote_copy(
            src_ref=out, dst_ref=into, send_sem=th_send.at[n], recv_sem=th_recv.at[n],
            device_id=(gx(dx), gy(dy)), device_id_type=MESH))
    for copy in halos:
        copy.start()

    for copy in winds:
        copy.wait_recv()
    for copy in requests:
        copy.wait_recv()
    odd = (lane & 1) == 1
    ends = jnp.logical_or(lane == 0, lane == 127)
    is_first = i == 0
    is_last = i == G - 1
    south_ok = jnp.where(j > 0, 1.0, 0.0).astype(F32)
    north_ok = jnp.where(j < H - 1, 1.0, 0.0).astype(F32)
    west_ok = jnp.where(i > 0, 1.0, 0.0).astype(F32)
    east_ok = jnp.where(i < G - 1, 1.0, 0.0).astype(F32)

    def both(south, north):
        return jnp.where(odd, north * north_ok, south * south_ok)

    def unpack(mixed, n):
        return pltpu.roll(mixed, (127 - 2 * n) % 128, 1)

    sub = iota((8, 128), 0)
    here = both(yw_in[0], yw_in[1])
    east = both(yw_in[2], yw_in[3]) * east_ok
    west = both(yw_in[4], yw_in[5]) * west_ok
    surface = []
    for c, source in ((0, uu), (1, vv)):
        zeros = jnp.zeros((8, 128), F32)
        left = [source[0]]
        right = [jnp.where(ends, unpack(here, 8 * c + g), 0.0) for g in range(8)]
        east_row = req_in[G - 1, 2 + c:3 + c, :] * east_ok
        west_row = req_in[1, 2 + c:3 + c, :] * west_ok
        left.append(jnp.where(sub == 0, east_row, 0.0))
        left += [zeros] * 6
        left.append(jnp.where(sub == 7, west_row, 0.0))
        right.append(jnp.where(jnp.logical_and(ends, sub == 0), unpack(east, 8 * c), 0.0))
        right += [zeros] * 6
        right.append(jnp.where(jnp.logical_and(ends, sub == 7), unpack(west, 8 * c + 7), 0.0))
        surface.append(jnp.concatenate(
            [jnp.concatenate(left, axis=0), jnp.concatenate(right, axis=0)], axis=1))

    lane_q = iota((16, 128), 1)
    k_q = iota((16, 128), 0)
    pick = ([], [])
    masks = []
    later = []
    for q in range(Q):
        place = req_in[q // CAP, q % CAP:q % CAP + 1, :].astype(jnp.int32)
        x0 = (place >> 5) * TA
        y0 = (place & 31) * TA
        for c in range(2):
            m = k_q - 6 * c
            hit = jnp.logical_and(
                lane_q == ((x0 - 1 + m) & 127), jnp.logical_and(m >= 0, m < 6))
            pick[c].append(jnp.where(hit, 1.0, 0.0))
        low = (lane_q - (y0 - 1)) & 255
        high = (lane_q + 128 - (y0 - 1)) & 255
        masks.append(jnp.concatenate(
            [jnp.where(low < 6, 1.0, 0.0), jnp.where(high < 6, 1.0, 0.0)], axis=1))
        later.append(jnp.broadcast_to((y0 & 4) != 0, (16, 128)))
    found = (dot_left_exact(jnp.concatenate(pick[0], axis=0), surface[0])
             + dot_left_exact(jnp.concatenate(pick[1], axis=0), surface[1]))
    found = found * jnp.concatenate(masks, axis=0)
    c_e = iota((256, 256), 0)
    l_e = iota((256, 256), 1)
    shift = jnp.where(l_e < 128, 1, 5)
    squeeze = jnp.where(((c_e + shift) & 7) == (l_e & 7), 1.0, 0.0)
    tight = dot_right_exact(found, squeeze)
    own_lanes = (lane_q >> 3) == k_q
    for q in range(Q):
        block = tight[16 * q:16 * q + 16]
        chosen = jnp.where(later[q], block[:, 128:], block[:, :128])
        rep_out[q // CAP, q % CAP:q % CAP + 1, :] = jnp.sum(
            jnp.where(own_lanes, chosen, 0.0), axis=0, keepdims=True)
    replies = [
        to_peer(-o, rep_out.at[o], rep_in.at[o], rep_send.at[o], rep_recv.at[o])
        for o in range(1, G)
    ]
    for copy in replies:
        copy.start()
    rep_in[0] = rep_out[0]

    def advect(zz, carry):
        rows_of = pl.ds(pl.multiple_of(zz * 8, 8), 8)
        mixed = both(yth_in[0, rows_of, :], yth_in[1, rows_of, :])
        for zl in range(GROUP):
            z = zz * GROUP + zl
            th[z, 7:8, :] = xth_in[0, pl.ds(z, 1), :] * west_ok
            th[z, 8 + BX:9 + BX, :] = xth_in[1, pl.ds(z, 1), :] * east_ok
            for g in range(8):
                at = 8 + 8 * g
                centre = th[z, at:at + 8, :]
                before = th[z, at - 1:at + 7, :]
                after = th[z, at + 1:at + 9, :]
                edge = unpack(mixed, zl * 8 + g)
                south = pltpu.roll(jnp.where(lane == 127, edge, centre), 1, 1)
                north = pltpu.roll(jnp.where(lane == 0, edge, centre), 127, 1)
                u = uu[z, 8 * g:8 * g + 8, :]
                v = vv[z, 8 * g:8 * g + 8, :]
                total = (jnp.maximum(u, 0.0) * (centre - before)
                         + jnp.minimum(u, 0.0) * (after - centre)
                         + jnp.maximum(v, 0.0) * (centre - south)
                         + jnp.minimum(v, 0.0) * (north - centre))
                part[z, 8 * g:8 * g + 8, :] = centre - 0.4 * total
        store(zz).start()
        return carry

    def store(zz):
        levels = pl.ds(zz * GROUP, GROUP)
        return pltpu.make_async_copy(part.at[levels], part_hbm.at[levels], part_sem.at[zz])

    groups = LZ // GROUP
    first_groups = groups // 2
    for copy in halos:
        copy.wait_recv()
    loads[3].wait()
    loads[4].wait()
    lax.fori_loop(0, first_groups, advect, 0)

    for copy in replies:
        copy.wait_recv()
    answers = jnp.concatenate([rep_in[o] for o in range(G)], axis=0)
    is_slot = jnp.where(code_col[:, :Q] == iota((TPD, Q), 1), 1.0, 0.0)
    patch = dot_left_exact(is_slot, answers)
    spread = jnp.concatenate(
        [jnp.where(own_lanes, patch[t:t + 1], 0.0) for t in range(TPD)], axis=0)
    by_y = jnp.where(
        (iota((128, 128), 0) & 7) < 6,
        interp_weight(iota((128, 128), 1), iota((128, 128), 0) & 7), 0.0)
    along_y = dot_right_exact(spread, by_y)
    high, middle, low = pieces(along_y)
    for t in range(TPD):
        small[t, 0:16, :] = high[16 * t:16 * t + 16]
        small[t, 16:32, :] = middle[16 * t:16 * t + 16]
        small[t, 32:48, :] = low[16 * t:16 * t + 16]

    for load in loads[5:]:
        load.wait()
    pair = 2
    lane_c = iota((R, 128), 1)
    first_lane = lane_c == 0
    last_lane = lane_c == 127

    def level_store(t):
        return pltpu.make_async_copy(
            lev.at[t, 8:8 + S, :], level_out.at[0, 0, t], lev_sem.at[t])

    def fuel_store(t):
        return pltpu.make_async_copy(fout.at[t], fuel_out.at[0, 0, t], fuel_sem.at[t])

    def fire(step, carry):
        for p in range(pair):
            t = step * pair + p
            wind[p] = dot(wide[...], small[t])
            lev[t, 7:8, :] = lev[t, 8:9, :]
            lev[t, 8 + S:9 + S, :] = lev[t, 7 + S:8 + S, :]
        for k in range(KSUB):
            for p in range(pair):
                t = step * pair + p
                old = lev.at[t] if k % 2 == 0 else spare.at[p]
                new = spare.at[p] if k % 2 == 0 else lev.at[t]
                for b in range(S // R):
                    at = 8 + R * b
                    centre = old[at:at + R, :]
                    before = old[at - 1:at - 1 + R, :]
                    after = old[at + 1:at + 1 + R, :]
                    left = jnp.where(first_lane, centre, pltpu.roll(centre, 1, 1))
                    right = jnp.where(last_lane, centre, pltpu.roll(centre, 127, 1))
                    dx = after - before
                    dy = right - left
                    around = (after + before) + (right + left)
                    square = dx * dx + dy * dy + 0.04
                    length = square * lax.rsqrt(square)
                    blown = (wind[p, R * b:R * b + R, :] * dx
                             + wind[p, S + R * b:S + R * b + R, :] * dy)
                    rate = (0.015 * base[t, R * b:R * b + R, :]) * jnp.maximum(
                        length + blown, 0.0)
                    level = (0.4 * centre + 0.15 * around) - rate
                    new[at:at + R, :] = level
                    if k < KSUB - 1:
                        if b == 0:
                            new[7:8, :] = level[0:1]
                        if b == S // R - 1:
                            new[8 + S:9 + S, :] = level[R - 1:R]
                    before_fuel = (fin if k == 0 else fout)[t, R * b:R * b + R, :]
                    fuel = before_fuel * (0.925 + 0.075 * jnp.tanh(level))
                    fout[t, R * b:R * b + R, :] = fuel
                    if k == KSUB - 1:
                        burnt = fin[t, R * b:R * b + R, :] - fuel
                        rows[b, pl.ds(t, 1), :] = jnp.sum(burnt, axis=0, keepdims=True)
        for p in range(pair):
            t = step * pair + p
            level_store(t).start()
            fuel_store(t).start()
        return carry

    lax.fori_loop(0, TPD // pair, fire, 0)

    l_m = iota((128, 128), 0)
    c_m = iota((128, 128), 1)
    mean = jnp.where((l_m >> 5) == (c_m & 3), 1.0 / (R * R), 0.0)
    fluxes = dot_right_exact(jnp.concatenate([rows[b] for b in range(TA)], axis=0), mean)
    slot_rows = iota((Q * TA, 64), 0)
    slot_lanes = iota((Q * TA, 64), 1)
    to_slot = jnp.where(
        jnp.logical_and(code_row[0:1, :64] == (slot_rows >> 2),
                        (slot_lanes >> 4) == (slot_rows & 3)), 1.0, 0.0)
    sent = dot_left_exact(to_slot, fluxes)
    for o in range(G):
        flux_out[o] = sent[8 * o:8 * o + 8]
    returned = [
        to_peer(o, flux_out.at[o], flux_in.at[o], flux_send.at[o], flux_recv.at[o])
        for o in range(1, G)
    ]
    for copy in returned:
        copy.start()
    flux_in[0] = flux_out[0]

    lax.fori_loop(first_groups, groups, advect, 0)

    lane8 = lane
    row8 = sub
    where_x = []
    where_y = []
    for o in range(G):
        p0 = req_in[o, 0:1, :].astype(jnp.int32)
        p1 = req_in[o, 1:2, :].astype(jnp.int32)
        place = jnp.where(row8 < TA, p0, p1)
        x0 = (place >> 5) * TA
        where_x.append(jnp.where(lane8 == x0 + (row8 & 3), 1.0, 0.0))
        where_y.append((lane8 >> 2) == (place & 31))
    across = jnp.concatenate(where_x, axis=0).T
    for copy in returned:
        copy.wait_recv()
    values = jnp.concatenate(
        [jnp.where(where_y[o], flux_in[o], 0.0) for o in range(G)], axis=0)
    field_ref[...] = dot_left_exact(across, values)[:BX]

    for copy in requests + winds + halos + replies + returned:
        copy.wait_send()

    def finish_tile(t, carry):
        level_store(t).wait()
        fuel_store(t).wait()
        return carry

    lax.fori_loop(0, TPD, finish_tile, 0)

    def finish_group(zz, carry):
        store(zz).wait()
        return carry

    lax.fori_loop(0, groups, finish_group, 0)


def body(G, H, theta, wind_u, wind_v, level_set, fuel_load, spread_base, tile_owner, tile_place):
    LZ = theta.shape[0]
    assert theta.shape[1:] == (BX, BY) and level_set.shape[2:] == (TPD, S, S)
    anywhere = pl.BlockSpec(memory_space=pl.ANY)
    scalars = pl.BlockSpec(memory_space=pltpu.SMEM)
    vmem = pl.BlockSpec(memory_space=pltpu.VMEM)
    dma = pltpu.SemaphoreType.DMA
    scratch = [
        pltpu.VMEM((LZ, BX + 16, BY), F32),
        pltpu.VMEM((LZ, BX, BY), F32),
        pltpu.VMEM((LZ, BX, BY), F32),
        pltpu.VMEM((LZ, BX, BY), F32),
        pltpu.VMEM((TPD, S + 16, S), F32),
        pltpu.VMEM((2, S + 16, S), F32),
        pltpu.VMEM((TPD, S, S), F32),
        pltpu.VMEM((TPD, S, S), F32),
        pltpu.VMEM((TPD, S, S), F32),
        pltpu.VMEM((2, 2 * S, S), F32),
        pltpu.VMEM((2 * S, 48), BF16),
        pltpu.VMEM((TPD, 48, S), BF16),
        pltpu.VMEM((TA, TPD, S), F32),
        pltpu.VMEM((TPD, 128), jnp.int32),
        pltpu.VMEM((G, 4, 128), F32),
        pltpu.VMEM((G, 4, 128), F32),
        pltpu.VMEM((G, 2, 128), F32),
        pltpu.VMEM((G, 2, 128), F32),
        pltpu.VMEM((G, 8, 128), F32),
        pltpu.VMEM((G, 8, 128), F32),
        pltpu.VMEM((8, 128), F32),
        pltpu.VMEM((6, 8, 128), F32),
        pltpu.VMEM((LZ, 128), F32),
        pltpu.VMEM((2, LZ, 128), F32),
        pltpu.VMEM((2, LZ, 128), F32),
        pltpu.VMEM((2, LZ, 128), F32),
        dma((8,)), dma((TPD,)), dma((TPD,)), dma((LZ // GROUP,)),
        dma((G,)), dma((G,)), dma((G,)), dma((G,)), dma((G,)), dma((G,)),
        dma((6,)), dma((6,)), dma((4,)), dma((4,)),
    ]
    part, level_next, fuel_next, field = pl.pallas_call(
        functools.partial(kernel, G, H, LZ),
        out_shape=(
            jax.ShapeDtypeStruct(theta.shape, F32),
            jax.ShapeDtypeStruct(level_set.shape, F32),
            jax.ShapeDtypeStruct(level_set.shape, F32),
            jax.ShapeDtypeStruct((BX, BY), F32),
        ),
        in_specs=[anywhere] * 6 + [scalars] * 2,
        out_specs=(anywhere, anywhere, anywhere, vmem),
        scratch_shapes=scratch,
        compiler_params=pltpu.CompilerParams(
            collective_id=0, has_side_effects=True, vmem_limit_bytes=40 * 1024 * 1024),
    )(theta, wind_u, wind_v, level_set, fuel_load, spread_base, tile_owner, tile_place)
    profile = 2.0 * jnp.exp(-(jnp.arange(LZ, dtype=F32) + 0.5) / (LZ / 4.0))
    theta_next = part + field[None, :, :] * profile[:, None, None]
    return (theta_next, level_next, fuel_next)


def solution(mesh):
    columns = P(None, "gx", "gy")
    tiles = P("gx", "gy", None, None, None)
    lists = P("gx", "gy", None)
    return jax.shard_map(
        functools.partial(body, mesh.shape["gx"], mesh.shape["gy"]),
        mesh=mesh,
        in_specs=(columns, columns, columns, tiles, tiles, tiles, lists, lists),
        out_specs=(columns, tiles, tiles),
        check_vma=False,
    )
```

time: 197 us -> 52.2 us (0.26)
  starting transfers between devices: 47.9 us -> 0 us
  other arithmetic: 47.2 us -> 1.78 us
  local copies, waits for them, and re-layouts: 54.4 us -> 10.4 us
  Pallas kernels: 0 us -> 39 us
  waiting for transfers between devices: 37.2 us -> 0 us
  matrix products: 7.96 us -> 0 us
    pallas_call x0 -> x1, Pallas kernels: none -> 39 us  [body(): pl.pallas_call(functools.partial(kernel, G, H, LZ), out_shape=(jax.ShapeD...]
    gather x50 -> x0, local copies, waits for them, and re-layouts: 34.1 us -> none
    all_to_all x3 -> x0, waiting for transfers between devices: 27 us -> none  [the longest x1 17.9 us: body(): lax.all_to_all(fine_wind.reshape(cycle, CAP, 2, S, S), 'gx', split_axis=0...]
    all_to_all x3 -> x0, starting transfers between devices: 27 us -> none  [the longest x1 15.4 us: body(): lax.all_to_all(outbox, 'gx', split_axis=0, concat_axis=0, tiled=True)]
    add x8 -> x1, other arithmetic: 25.3 us -> 1.77 us  [body(): theta_next = part + field[None, :, :] * profile[:, None, None]]
    ppermute x8 -> x0, starting transfers between devices: 20.9 us -> none  [the longest x4 15.5 us: padded_2(): lax.ppermute(tail, axis, [(i, (i + 1) % count) for i in range(ends)])]
    scatter-add x1 -> x0, other arithmetic: 12.8 us -> none  [body(): jnp.zeros((cells_x, cells_y), jnp.float32).at[index_x, index_y]]
    slice x19 -> x0, local copies, waits for them, and re-layouts: 12.4 us -> none  [the longest x4 5.45 us: padded_2(): lax.slice_in_dim(cells, cells.shape[dim] - width, cells.shape[dim], axis=...]
  transfers between devices with their start and end apart: 11 -> 0, of which waited for: 5 -> 0; matrix products, arithmetic and copies ran while one was open for 23% -> 0% of each run, Pallas kernels for 0% -> 0%
where the time goes in v1:
time: 52.2 us; the launch traced here: 51.9 us
  Pallas kernels  39 us (75%)
  local copies, waits for them, and re-layouts  10.4 us (20%)
  other arithmetic  1.78 us (3%)
  between operations  0.66 us (1%)
    pallas_call x1, Pallas kernels, body(): pl.pallas_call(functools.partial(kernel, G, H, LZ), out_shape=(jax.ShapeD...  39 us
    unnamed x16, local copies, waits for them, and re-layouts  10.4 us
    add x1, other arithmetic, body(): theta_next = part + field[None, :, :] * profile[:, None, None]  1.77 us

profile of v1, /device:TPU:0, one launch (start us, length us, event | category | flops | bytes accessed | tf_op | source)
XLA Modules:
  0.0 51.9 jit_solution(4870884389263348646)
XLA Ops:
  0.6 0.0 copy-start
  0.7 1.7 %copy-done = f32[80,64,128]{2,1,0:T(8,128)S(1)} copy-done((f32[80,64,128]{2,1,0:T(8,128)S(1)}, f32[80,64,128]{2,1,0:T(8,128)}, u32[]{:S(2)}) %copy-start) | copy-done | bytes 2621464
  2.4 0.0 copy-start.1
  2.4 1.7 %copy-done.1 = f32[80,64,128]{2,1,0:T(8,128)S(1)} copy-done((f32[80,64,128]{2,1,0:T(8,128)S(1)}, f32[80,64,128]{2,1,0:T(8,128)}, u32[]{:S(2)}) %copy-start.1) | copy-done | bytes 2621464
  4.1 0.0 copy-start.2
  4.1 1.2 %copy-done.2 = f32[1,1,16,128,128]{4,3,2,1,0:T(8,128)S(1)} copy-done((f32[1,1,16,128,128]{4,3,2,1,0:T(8,128)S(1)}, f32[1,1,16,128,128]{4,3,2,1,0:T(8,128)}, u32[]{:S(2)}) %copy-start.2) | copy-done | bytes 1048600
  5.4 0.0 copy-start.3
  5.4 1.2 %copy-done.3 = f32[1,1,16,128,128]{4,3,2,1,0:T(8,128)S(1)} copy-done((f32[1,1,16,128,128]{4,3,2,1,0:T(8,128)S(1)}, f32[1,1,16,128,128]{4,3,2,1,0:T(8,128)}, u32[]{:S(2)}) %copy-start.3) | copy-done | bytes 1048600
  6.6 0.0 copy-start.4
  6.6 1.2 %copy-done.4 = f32[1,1,16,128,128]{4,3,2,1,0:T(8,128)S(1)} copy-done((f32[1,1,16,128,128]{4,3,2,1,0:T(8,128)S(1)}, f32[1,1,16,128,128]{4,3,2,1,0:T(8,128)}, u32[]{:S(2)}) %copy-start.4) | copy-done | bytes 1048600
  7.8 0.0 copy-start.5
  7.8 0.7 %copy-done.5 = s32[1,1,16]{2,1,0:T(1,128)S(1)} copy-done((s32[1,1,16]{2,1,0:T(1,128)S(1)}, s32[1,1,16]{2,1,0:T(1,128)}, u32[]{:S(2)}) %copy-start.5) | copy-done | bytes 88
  8.5 0.0 copy-start.6
  8.5 0.7 %copy-done.6 = s32[1,1,16]{2,1,0:T(1,128)S(1)} copy-done((s32[1,1,16]{2,1,0:T(1,128)S(1)}, s32[1,1,16]{2,1,0:T(1,128)}, u32[]{:S(2)}) %copy-start.6) | copy-done | bytes 88
  9.1 39.0 %shard_map.103 = (f32[80,64,128]{2,1,0:T(8,128)S(1)}, f32[1,1,16,128,128]{4,3,2,1,0:T(8,128)S(1)}, f32[1,1,16,128,128]{4,3,2,1,0:T(8,128)S(1)}, f32[64,128]{1,0:T(8,128)S(1)}) custom-call(f32[80,64,128]{2,1,0:T(8,128)S(1)} %copy-done, f32[80,64,128]{2,1,0:T(8,128)S(1)} %copy-done.1, f32[80,64,128]{2,1,0:T(8,128)} %v_hbm.1, ...), custom_call_target="tpu_custom_call" | custom-call | tf_op jit(solution)/shard_map/pallas_call | solution.py:494
  48.2 1.8 %multiply_add_fusion = f32[80,64,128]{2,1,0:T(8,128)} fusion(f32[80,64,128]{2,1,0:T(8,128)S(1)} %get-tuple-element.7, f32[80]{0:T(128)S(1)} %exponential_multiply_fusion, f32[64,128]{1,0:T(8,128)S(1)} %get-tuple-element.8), kind=kLoop, calls=%fused_computation | loop fusion | flops 1310720 | bytes 5275968 | tf_op jit(solution)/shard_map/add | solution.py:509
  49.9 1.0 %copy.13 = f32[1,1,16,128,128]{4,3,2,1,0:T(8,128)} copy(f32[1,1,16,128,128]{4,3,2,1,0:T(8,128)S(1)} %get-tuple-element.15) | data formatting | bytes 2097152
  50.9 1.0 %copy.14 = f32[1,1,16,128,128]{4,3,2,1,0:T(8,128)} copy(f32[1,1,16,128,128]{4,3,2,1,0:T(8,128)S(1)} %get-tuple-element.16) | data formatting | bytes 2097152
  (1 shorter events, 0.0 us)
Async XLA Ops:
  0.6 1.7 %copy-start = (f32[80,64,128]{2,1,0:T(8,128)S(1)}, f32[80,64,128]{2,1,0:T(8,128)}, u32[]{:S(2)}) copy-start(f32[80,64,128]{2,1,0:T(8,128)} %theta_hbm.1) | copy-start | bytes 7864324
  2.4 1.7 %copy-start.1 = (f32[80,64,128]{2,1,0:T(8,128)S(1)}, f32[80,64,128]{2,1,0:T(8,128)}, u32[]{:S(2)}) copy-start(f32[80,64,128]{2,1,0:T(8,128)} %u_hbm.1) | copy-start | bytes 7864324
  4.1 1.2 %copy-start.2 = (f32[1,1,16,128,128]{4,3,2,1,0:T(8,128)S(1)}, f32[1,1,16,128,128]{4,3,2,1,0:T(8,128)}, u32[]{:S(2)}) copy-start(f32[1,1,16,128,128]{4,3,2,1,0:T(8,128)} %level_hbm.1) | copy-start | bytes 3145732
  5.4 1.2 %copy-start.3 = (f32[1,1,16,128,128]{4,3,2,1,0:T(8,128)S(1)}, f32[1,1,16,128,128]{4,3,2,1,0:T(8,128)}, u32[]{:S(2)}) copy-start(f32[1,1,16,128,128]{4,3,2,1,0:T(8,128)} %fuel_hbm.1) | copy-start | bytes 3145732
  6.6 1.2 %copy-start.4 = (f32[1,1,16,128,128]{4,3,2,1,0:T(8,128)S(1)}, f32[1,1,16,128,128]{4,3,2,1,0:T(8,128)}, u32[]{:S(2)}) copy-start(f32[1,1,16,128,128]{4,3,2,1,0:T(8,128)} %base_hbm.1) | copy-start | bytes 3145732
  7.8 0.7 %copy-start.5 = (s32[1,1,16]{2,1,0:T(1,128)S(1)}, s32[1,1,16]{2,1,0:T(1,128)}, u32[]{:S(2)}) copy-start(s32[1,1,16]{2,1,0:T(1,128)} %owner_ref.1) | copy-start | bytes 196
  8.5 0.7 %copy-start.6 = (s32[1,1,16]{2,1,0:T(1,128)S(1)}, s32[1,1,16]{2,1,0:T(1,128)}, u32[]{:S(2)}) copy-start(s32[1,1,16]{2,1,0:T(1,128)} %place_ref.1) | copy-start | bytes 196

commit v2 on v1

--- a/solution.py
+++ b/solution.py
@@ -57,9 +57,10 @@
 
 def kernel(
     G, H, LZ,
-    theta_hbm, u_hbm, v_hbm, level_hbm, fuel_hbm, base_hbm, owner_ref, place_ref,
+    theta_hbm, u_hbm, v_hbm, level_hbm, fuel_hbm, base_hbm, owner_hbm, place_hbm,
     part_hbm, level_out, fuel_out, field_ref,
-    th, uu, vv, part, lev, spare, fin, fout, base, wind, wide, small, rows, code_col,
+    th, uu, vv, part, lev, lout, ping, pong, fin, burn, fout, base, wind, scaled,
+    wide, small, rows, code_col, owner_ref, place_ref,
     req_out, req_in, rep_out, rep_in, flux_out, flux_in,
     yw_out, yw_in, yth_out, yth_in, xth_out, xth_in,
     in_sem, lev_sem, fuel_sem, part_sem,
@@ -77,6 +78,8 @@
         return lax.rem(j + (offset % H), H)
 
     loads = [
+        pltpu.make_async_copy(owner_hbm, owner_ref, in_sem.at[8]),
+        pltpu.make_async_copy(place_hbm, place_ref, in_sem.at[9]),
         pltpu.make_async_copy(u_hbm.at[0], uu.at[0], in_sem.at[0]),
         pltpu.make_async_copy(v_hbm.at[0], vv.at[0], in_sem.at[1]),
         pltpu.make_async_copy(theta_hbm, th.at[:, 8:8 + BX, :], in_sem.at[2]),
@@ -96,6 +99,8 @@
     for dx, dy in corners:
         pl.semaphore_signal(barrier, inc=1, device_id=(gx(dx), gy(dy)), device_id_type=MESH)
 
+    loads[0].wait()
+    loads[1].wait()
     lane = iota((8, 128), 1)
     lane16 = lane & (TPD - 1)
     sub16 = iota((TPD, 128), 0)
@@ -128,8 +133,8 @@
         place1 + 1, 0).astype(F32)
     asked = jnp.broadcast_to(jnp.sum(wanted, axis=1, keepdims=True) - 1.0, (Q, 128))
 
-    loads[0].wait()
-    loads[1].wait()
+    loads[2].wait()
+    loads[3].wait()
     for o in range(G):
         req_out[o, 0:2, :] = asked[2 * o:2 * o + 2]
         edge = 0 if o == G - 1 else BX - 1
@@ -171,7 +176,7 @@
         interp_weight(fine_of & (S - 1), column), 0.0).astype(BF16)
     wide[...] = a3
 
-    loads[2].wait()
+    loads[4].wait()
 
     def pack(zz, carry):
         acc = jnp.zeros((8, 128), F32)
@@ -285,8 +290,6 @@
         mixed = both(yth_in[0, rows_of, :], yth_in[1, rows_of, :])
         for zl in range(GROUP):
             z = zz * GROUP + zl
-            th[z, 7:8, :] = xth_in[0, pl.ds(z, 1), :] * west_ok
-            th[z, 8 + BX:9 + BX, :] = xth_in[1, pl.ds(z, 1), :] * east_ok
             for g in range(8):
                 at = 8 + 8 * g
                 centre = th[z, at:at + 8, :]
@@ -313,8 +316,17 @@
     first_groups = groups // 2
     for copy in halos:
         copy.wait_recv()
-    loads[3].wait()
-    loads[4].wait()
+    loads[5].wait()
+    loads[6].wait()
+
+    def rim(zz, carry):
+        for zl in range(GROUP):
+            z = zz * GROUP + zl
+            th[z, 7:8, :] = xth_in[0, pl.ds(z, 1), :] * west_ok
+            th[z, 8 + BX:9 + BX, :] = xth_in[1, pl.ds(z, 1), :] * east_ok
+        return carry
+
+    lax.fori_loop(0, groups, rim, 0)
     lax.fori_loop(0, first_groups, advect, 0)
 
     for copy in replies:
@@ -334,7 +346,7 @@
         small[t, 16:32, :] = middle[16 * t:16 * t + 16]
         small[t, 32:48, :] = low[16 * t:16 * t + 16]
 
-    for load in loads[5:]:
+    for load in loads[7:]:
         load.wait()
     pair = 2
     lane_c = iota((R, 128), 1)
@@ -342,25 +354,38 @@
     last_lane = lane_c == 127
 
     def level_store(t):
-        return pltpu.make_async_copy(
-            lev.at[t, 8:8 + S, :], level_out.at[0, 0, t], lev_sem.at[t])
+        return pltpu.make_async_copy(lout.at[t], level_out.at[0, 0, t], lev_sem.at[t])
 
     def fuel_store(t):
         return pltpu.make_async_copy(fout.at[t], fuel_out.at[0, 0, t], fuel_sem.at[t])
+
+    def pad_tile(t, carry):
+        lev[t, 7:8, :] = lev[t, 8:9, :]
+        lev[t, 8 + S:9 + S, :] = lev[t, 7 + S:8 + S, :]
+        return carry
+
+    lax.fori_loop(0, TPD, pad_tile, 0)
 
     def fire(step, carry):
         for p in range(pair):
             t = step * pair + p
             wind[p] = dot(wide[...], small[t])
-            lev[t, 7:8, :] = lev[t, 8:9, :]
-            lev[t, 8 + S:9 + S, :] = lev[t, 7 + S:8 + S, :]
+            for b in range(S // R):
+                strength = 0.015 * base[t, R * b:R * b + R, :]
+                scaled[p, R * b:R * b + R, :] = strength
+                wind[p, R * b:R * b + R, :] = wind[p, R * b:R * b + R, :] * strength
+                wind[p, S + R * b:S + R * b + R, :] = (
+                    wind[p, S + R * b:S + R * b + R, :] * strength)
         for k in range(KSUB):
+            last = k == KSUB - 1
             for p in range(pair):
                 t = step * pair + p
-                old = lev.at[t] if k % 2 == 0 else spare.at[p]
-                new = spare.at[p] if k % 2 == 0 else lev.at[t]
+                old = lev.at[t] if k == 0 else (ping, pong)[(k - 1) % 2].at[p]
+                new = (ping, pong)[k % 2].at[p]
+                fuel_old = fin.at[t] if k == 0 else burn.at[p]
                 for b in range(S // R):
                     at = 8 + R * b
+                    here_b = slice(R * b, R * b + R)
                     centre = old[at:at + R, :]
                     before = old[at - 1:at - 1 + R, :]
                     after = old[at + 1:at + 1 + R, :]
@@ -369,25 +394,25 @@
                     dx = after - before
                     dy = right - left
                     around = (after + before) + (right + left)
-                    square = dx * dx + dy * dy + 0.04
+                    square = (dx * dx + 0.04) + dy * dy
                     length = square * lax.rsqrt(square)
                     blown = (wind[p, R * b:R * b + R, :] * dx
                              + wind[p, S + R * b:S + R * b + R, :] * dy)
-                    rate = (0.015 * base[t, R * b:R * b + R, :]) * jnp.maximum(
-                        length + blown, 0.0)
+                    rate = jnp.maximum(scaled[p, here_b, :] * length + blown, 0.0)
                     level = (0.4 * centre + 0.15 * around) - rate
-                    new[at:at + R, :] = level
-                    if k < KSUB - 1:
+                    fuel = fuel_old[here_b, :] * (0.925 + 0.075 * jnp.tanh(level))
+                    if last:
+                        lout[t, here_b, :] = level
+                        fout[t, here_b, :] = fuel
+                        burnt = fin[t, here_b, :] - fuel
+                        rows[b, pl.ds(t, 1), :] = jnp.sum(burnt, axis=0, keepdims=True)
+                    else:
+                        new[at:at + R, :] = level
                         if b == 0:
                             new[7:8, :] = level[0:1]
                         if b == S // R - 1:
                             new[8 + S:9 + S, :] = level[R - 1:R]
-                    before_fuel = (fin if k == 0 else fout)[t, R * b:R * b + R, :]
-                    fuel = before_fuel * (0.925 + 0.075 * jnp.tanh(level))
-                    fout[t, R * b:R * b + R, :] = fuel
-                    if k == KSUB - 1:
-                        burnt = fin[t, R * b:R * b + R, :] - fuel
-                        rows[b, pl.ds(t, 1), :] = jnp.sum(burnt, axis=0, keepdims=True)
+                        burn[p, here_b, :] = fuel
         for p in range(pair):
             t = step * pair + p
             level_store(t).start()
@@ -453,11 +478,24 @@
     lax.fori_loop(0, groups, finish_group, 0)
 
 
+def finish(LZ, per_step, part, level, fuel, field, theta_next, level_next, fuel_next):
+    first = pl.program_id(0) * per_step
+    heat = 2.0 * field[...]
+    for n in range(per_step):
+        z = jnp.full((8, BY), first + n, jnp.int32).astype(F32)
+        profile = jnp.exp(-(z + 0.5) / (LZ / 4.0))
+        for g in range(BX // 8):
+            at = slice(8 * g, 8 * g + 8)
+            theta_next[n, at, :] = part[n, at, :] + heat[at] * profile
+    level_next[...] = level[...]
+    fuel_next[...] = fuel[...]
+
+
 def body(G, H, theta, wind_u, wind_v, level_set, fuel_load, spread_base, tile_owner, tile_place):
     LZ = theta.shape[0]
     assert theta.shape[1:] == (BX, BY) and level_set.shape[2:] == (TPD, S, S)
     anywhere = pl.BlockSpec(memory_space=pl.ANY)
-    scalars = pl.BlockSpec(memory_space=pltpu.SMEM)
+    far = pl.BlockSpec(memory_space=pltpu.HBM)
     vmem = pl.BlockSpec(memory_space=pltpu.VMEM)
     dma = pltpu.SemaphoreType.DMA
     scratch = [
@@ -466,15 +504,21 @@
         pltpu.VMEM((LZ, BX, BY), F32),
         pltpu.VMEM((LZ, BX, BY), F32),
         pltpu.VMEM((TPD, S + 16, S), F32),
+        pltpu.VMEM((TPD, S, S), F32),
+        pltpu.VMEM((2, S + 16, S), F32),
         pltpu.VMEM((2, S + 16, S), F32),
         pltpu.VMEM((TPD, S, S), F32),
+        pltpu.VMEM((2, S, S), F32),
         pltpu.VMEM((TPD, S, S), F32),
         pltpu.VMEM((TPD, S, S), F32),
         pltpu.VMEM((2, 2 * S, S), F32),
+        pltpu.VMEM((2, S, S), F32),
         pltpu.VMEM((2 * S, 48), BF16),
         pltpu.VMEM((TPD, 48, S), BF16),
         pltpu.VMEM((TA, TPD, S), F32),
         pltpu.VMEM((TPD, 128), jnp.int32),
+        pltpu.SMEM((1, 1, TPD), jnp.int32),
+        pltpu.SMEM((1, 1, TPD), jnp.int32),
         pltpu.VMEM((G, 4, 128), F32),
         pltpu.VMEM((G, 4, 128), F32),
         pltpu.VMEM((G, 2, 128), F32),
@@ -487,7 +531,7 @@
         pltpu.VMEM((2, LZ, 128), F32),
         pltpu.VMEM((2, LZ, 128), F32),
         pltpu.VMEM((2, LZ, 128), F32),
-        dma((8,)), dma((TPD,)), dma((TPD,)), dma((LZ // GROUP,)),
+        dma((10,)), dma((TPD,)), dma((TPD,)), dma((LZ // GROUP,)),
         dma((G,)), dma((G,)), dma((G,)), dma((G,)), dma((G,)), dma((G,)),
         dma((6,)), dma((6,)), dma((4,)), dma((4,)),
     ]
@@ -499,15 +543,28 @@
             jax.ShapeDtypeStruct(level_set.shape, F32),
             jax.ShapeDtypeStruct((BX, BY), F32),
         ),
-        in_specs=[anywhere] * 6 + [scalars] * 2,
+        in_specs=[far] * 8,
         out_specs=(anywhere, anywhere, anywhere, vmem),
         scratch_shapes=scratch,
         compiler_params=pltpu.CompilerParams(
-            collective_id=0, has_side_effects=True, vmem_limit_bytes=40 * 1024 * 1024),
+            collective_id=0, has_side_effects=True, vmem_limit_bytes=58 * 1024 * 1024),
     )(theta, wind_u, wind_v, level_set, fuel_load, spread_base, tile_owner, tile_place)
-    profile = 2.0 * jnp.exp(-(jnp.arange(LZ, dtype=F32) + 0.5) / (LZ / 4.0))
-    theta_next = part + field[None, :, :] * profile[:, None, None]
-    return (theta_next, level_next, fuel_next)
+    steps = 8
+    levels = pl.BlockSpec((LZ // steps, BX, BY), lambda n: (n, 0, 0))
+    two = pl.BlockSpec((1, 1, TPD // steps, S, S), lambda n: (0, 0, n, 0, 0))
+    whole = pl.BlockSpec((BX, BY), lambda n: (0, 0))
+    return pl.pallas_call(
+        functools.partial(finish, LZ, LZ // steps),
+        grid=(steps,),
+        out_shape=(
+            jax.ShapeDtypeStruct(theta.shape, F32),
+            jax.ShapeDtypeStruct(level_set.shape, F32),
+            jax.ShapeDtypeStruct(level_set.shape, F32),
+        ),
+        in_specs=[levels, two, two, whole],
+        out_specs=(levels, two, two),
+        compiler_params=pltpu.CompilerParams(vmem_limit_bytes=58 * 1024 * 1024),
+    )(part, level_next, fuel_next, field)
 
 
 def solution(mesh):

time: 52.2 us -> 43.2 us (0.83)
  local copies, waits for them, and re-layouts: 10.4 us -> 0 us
  Pallas kernels: 39 us -> 42.2 us
  other arithmetic: 1.78 us -> 0 us
    unnamed x16 -> x0, local copies, waits for them, and re-layouts: 10.4 us -> none
    pallas_call x0 -> x1, Pallas kernels: none -> 6.82 us  [body(): pl.pallas_call(functools.partial(finish, LZ, LZ // steps), grid=(steps,),...]
    pallas_call x1, Pallas kernels: 39 us -> 35.4 us  [body(): pl.pallas_call(functools.partial(kernel, G, H, LZ), out_shape=(jax.ShapeD...]
    add x1 -> x0, other arithmetic: 1.77 us -> none  [body(): theta_next = part + field[None, :, :] * profile[:, None, None]]
where the time goes in v2:
time: 43.2 us; the launch traced here: 42.9 us
  Pallas kernels  42.2 us (98%)
  between operations  0.64 us (1%)
    pallas_call x1, Pallas kernels, body(): pl.pallas_call(functools.partial(kernel, G, H, LZ), out_shape=(jax.ShapeD...  35.4 us
    pallas_call x1, Pallas kernels, body(): pl.pallas_call(functools.partial(finish, LZ, LZ // steps), grid=(steps,),...  6.82 us

profile of v2, /device:TPU:0, one launch (start us, length us, event | category | flops | bytes accessed | tf_op | source)
XLA Modules:
  0.0 42.9 jit_solution(14085346578243903802)
XLA Ops:
  0.6 35.4 %shard_map.103 = (f32[80,64,128]{2,1,0:T(8,128)}, f32[1,1,16,128,128]{4,3,2,1,0:T(8,128)}, f32[1,1,16,128,128]{4,3,2,1,0:T(8,128)}, f32[64,128]{1,0:T(8,128)}) custom-call(f32[80,64,128]{2,1,0:T(8,128)} %theta_hbm.1, f32[80,64,128]{2,1,0:T(8,128)} %u_hbm.1, f32[80,64,128]{2,1,0:T(8,128)} %v_hbm.1, f32[1,1,16,128,128]{4,3,2,1,0:T(8,128)} %level_hbm.1, ...), custom_call_target="tpu_custom_call" | custom-call | tf_op jit(solution)/shard_map/pallas_call | solution.py:538
  36.1 6.8 %shard_map.104 = (f32[80,64,128]{2,1,0:T(8,128)}, f32[1,1,16,128,128]{4,3,2,1,0:T(8,128)}, f32[1,1,16,128,128]{4,3,2,1,0:T(8,128)}) custom-call(f32[80,64,128]{2,1,0:T(8,128)} %get-tuple-element.7.part, f32[1,1,16,128,128]{4,3,2,1,0:T(8,128)} %get-tuple-element.8.level, f32[1,1,16,128,128]{4,3,2,1,0:T(8,128)} %get-tuple-element.9.fuel, ...), custom_call_target="tpu_custom_call" | custom-call | tf_op jit(solution)/shard_map/pallas_call | solution.py:556

commit v3 on v1

v3 whole, which is shorter than its diff:
```python
import functools

import jax
import jax.numpy as jnp
from jax import lax
from jax.experimental import pallas as pl
from jax.experimental.pallas import tpu as pltpu
from jax.sharding import PartitionSpec as P

TA = 4
R = 32
KSUB = 6
CAP = 2
TPD = 16
S = 128
BX = 64
BY = 128
GROUP = 8
PAIR = 2
LIMITS = (48, 24, 24)

MESH = pl.DeviceIdType.MESH
F32 = jnp.float32
BF16 = jnp.bfloat16


def iota(shape, dim):
    return lax.broadcasted_iota(jnp.int32, shape, dim)


def pieces(x):
    high = x.astype(BF16)
    rest = x - high.astype(F32)
    middle = rest.astype(BF16)
    low = (rest - middle.astype(F32)).astype(BF16)
    return (high, middle, low)


def dot(a, b):
    return jnp.dot(a, b, preferred_element_type=F32)


def dot_left_exact(a, b):
    a = a.astype(BF16)
    high, middle, low = pieces(b)
    return dot(a, high) + (dot(a, middle) + dot(a, low))


def dot_right_exact(a, b):
    b = b.astype(BF16)
    high, middle, low = pieces(a)
    return dot(high, b) + (dot(middle, b) + dot(low, b))


def interp_weight(fine, column):
    where_fine = (fine.astype(F32) + 0.5) / R + 0.5
    return jnp.maximum(0.0, 1.0 - jnp.abs(where_fine - column.astype(F32)))


def exchange(
    G, H, LZ,
    theta_hbm, u_hbm, v_hbm, owner_hbm, place_hbm,
    small, code_out, asked_out, ymix, xhalo,
    th, u_low, v_low, code_col, owner_ref, place_ref,
    req_out, req_in, rep_out, rep_in,
    yw_out, yw_in, yth_out, yth_in, xth_out, xth_in,
    in_sem,
    req_send, req_recv, rep_send, rep_recv,
    yw_send, yw_recv, th_send, th_recv,
):
    Q = G * CAP
    i = lax.axis_index("gx")
    j = lax.axis_index("gy")

    def gx(offset):
        return lax.rem(i + (offset % G), G)

    def gy(offset):
        return lax.rem(j + (offset % H), H)

    loads = [
        pltpu.make_async_copy(owner_hbm, owner_ref, in_sem.at[0]),
        pltpu.make_async_copy(place_hbm, place_ref, in_sem.at[1]),
        pltpu.make_async_copy(u_hbm.at[0], u_low, in_sem.at[2]),
        pltpu.make_async_copy(v_hbm.at[0], v_low, in_sem.at[3]),
        pltpu.make_async_copy(theta_hbm, th, in_sem.at[4]),
    ]
    for load in loads:
        load.start()

    corners = [(0, 1), (0, -1), (-1, 1), (-1, -1), (1, 1), (1, -1)]
    barrier = pltpu.get_barrier_semaphore()
    for o in range(1, G):
        pl.semaphore_signal(barrier, inc=1, device_id=(gx(o), j), device_id_type=MESH)
    for dx, dy in corners:
        pl.semaphore_signal(barrier, inc=1, device_id=(gx(dx), gy(dy)), device_id_type=MESH)

    loads[0].wait()
    loads[1].wait()
    lane = iota((8, 128), 1)
    lane16 = lane & (TPD - 1)
    sub16 = iota((TPD, 128), 0)
    own_row = jnp.zeros((8, 128), jnp.int32)
    place_row = jnp.zeros((8, 128), jnp.int32)
    own_col = jnp.zeros((TPD, 128), jnp.int32)
    for t in range(TPD):
        own_row = jnp.where(lane16 == t, owner_ref[0, 0, t], own_row)
        place_row = jnp.where(lane16 == t, place_ref[0, 0, t], place_row)
        own_col = jnp.where(sub16 == t, owner_ref[0, 0, t], own_col)
    rank_row = jnp.zeros((8, 128), jnp.int32)
    rank_col = jnp.zeros((TPD, 128), jnp.int32)
    for t in range(TPD):
        rank_row += jnp.where(
            jnp.logical_and(own_row == owner_ref[0, 0, t], lane16 > t), 1, 0)
        rank_col += jnp.where(
            jnp.logical_and(own_col == owner_ref[0, 0, t], sub16 > t), 1, 0)

    def code_of(owner, rank):
        away = owner - i
        return jnp.where(away < 0, away + G, away) * CAP + rank

    code_row = code_of(own_row, rank_row)
    code_out[...] = code_row
    code_col[...] = code_of(own_col, rank_col)

    row1 = code_row[0:1]
    place1 = place_row[0:1]
    wanted = jnp.where(
        jnp.logical_and(row1 == iota((Q, 128), 0), iota((Q, 128), 1) < TPD),
        place1 + 1, 0).astype(F32)
    asked = jnp.broadcast_to(jnp.sum(wanted, axis=1, keepdims=True) - 1.0, (Q, 128))

    loads[2].wait()
    loads[3].wait()
    for o in range(G):
        req_out[o, 0:2, :] = asked[2 * o:2 * o + 2]
        edge = 0 if o == G - 1 else BX - 1
        req_out[o, 2:3, :] = u_low[edge:edge + 1, :]
        req_out[o, 3:4, :] = v_low[edge:edge + 1, :]
    packed = jnp.zeros((8, 128), F32)
    for g in range(16):
        source = u_low if g < 8 else v_low
        cell = source[8 * (g % 8):8 * (g % 8) + 8, :]
        packed = jnp.where((lane >> 1) == g, pltpu.roll(cell, 2 * g + 1, 1), packed)
    yw_out[...] = packed

    pl.semaphore_wait(barrier, G - 1 + len(corners))

    def to_peer(o, out, into, send, recv):
        return pltpu.make_async_remote_copy(
            src_ref=out, dst_ref=into, send_sem=send, recv_sem=recv,
            device_id=(gx(o), j), device_id_type=MESH)

    requests = [
        to_peer(o, req_out.at[o], req_in.at[o], req_send.at[o], req_recv.at[o])
        for o in range(1, G)
    ]
    winds = [
        pltpu.make_async_remote_copy(
            src_ref=yw_out, dst_ref=yw_in.at[n], send_sem=yw_send.at[n],
            recv_sem=yw_recv.at[n], device_id=(gx(dx), gy(dy)), device_id_type=MESH)
        for n, (dx, dy) in enumerate(corners)
    ]
    for copy in requests + winds:
        copy.start()
    req_in[0] = req_out[0]

    loads[4].wait()

    def pack(zz, carry):
        acc = jnp.zeros((8, 128), F32)
        for zl in range(GROUP):
            z = zz * GROUP + zl
            for g in range(8):
                n = zl * 8 + g
                cell = th[z, 8 * g:8 * g + 8, :]
                acc = jnp.where((lane >> 1) == n, pltpu.roll(cell, (2 * n + 1) % 128, 1), acc)
            xth_out[0, pl.ds(z, 1), :] = th[z, BX - 1:BX, :]
            xth_out[1, pl.ds(z, 1), :] = th[z, 0:1, :]
        yth_out[pl.ds(pl.multiple_of(zz * 8, 8), 8), :] = acc
        return carry

    lax.fori_loop(0, LZ // GROUP, pack, 0)
    halos = []
    for n, (out, into, dx, dy) in enumerate([
        (xth_out.at[0], xth_in.at[0], 1, 0),
        (xth_out.at[1], xth_in.at[1], -1, 0),
        (yth_out, yth_in.at[0], 0, 1),
        (yth_out, yth_in.at[1], 0, -1),
    ]):
        halos.append(pltpu.make_async_remote_copy(
            src_ref=out, dst_ref=into, send_sem=th_send.at[n], recv_sem=th_recv.at[n],
            device_id=(gx(dx), gy(dy)), device_id_type=MESH))
    for copy in halos:
        copy.start()

    for copy in winds:
        copy.wait_recv()
    for copy in requests:
        copy.wait_recv()
    odd = (lane & 1) == 1
    ends = jnp.logical_or(lane == 0, lane == 127)
    south_ok = jnp.where(j > 0, 1.0, 0.0).astype(F32)
    north_ok = jnp.where(j < H - 1, 1.0, 0.0).astype(F32)
    west_ok = jnp.where(i > 0, 1.0, 0.0).astype(F32)
    east_ok = jnp.where(i < G - 1, 1.0, 0.0).astype(F32)

    def both(south, north):
        return jnp.where(odd, north * north_ok, south * south_ok)

    def unpack(mixed, n):
        return pltpu.roll(mixed, (127 - 2 * n) % 128, 1)

    sub = iota((8, 128), 0)
    here = both(yw_in[0], yw_in[1])
    east = both(yw_in[2], yw_in[3]) * east_ok
    west = both(yw_in[4], yw_in[5]) * west_ok
    surface = []
    for c, source in ((0, u_low), (1, v_low)):
        zeros = jnp.zeros((8, 128), F32)
        left = [source[...]]
        right = [jnp.where(ends, unpack(here, 8 * c + g), 0.0) for g in range(8)]
        east_row = req_in[G - 1, 2 + c:3 + c, :] * east_ok
        west_row = req_in[1, 2 + c:3 + c, :] * west_ok
        left.append(jnp.where(sub == 0, east_row, 0.0))
        left += [zeros] * 6
        left.append(jnp.where(sub == 7, west_row, 0.0))
        right.append(jnp.where(jnp.logical_and(ends, sub == 0), unpack(east, 8 * c), 0.0))
        right += [zeros] * 6
        right.append(jnp.where(jnp.logical_and(ends, sub == 7), unpack(west, 8 * c + 7), 0.0))
        surface.append(jnp.concatenate(
            [jnp.concatenate(left, axis=0), jnp.concatenate(right, axis=0)], axis=1))

    lane_q = iota((16, 128), 1)
    k_q = iota((16, 128), 0)
    pick = ([], [])
    masks = []
    later = []
    for q in range(Q):
        place = req_in[q // CAP, q % CAP:q % CAP + 1, :].astype(jnp.int32)
        x0 = (place >> 5) * TA
        y0 = (place & 31) * TA
        for c in range(2):
            m = k_q - 6 * c
            hit = jnp.logical_and(
                lane_q == ((x0 - 1 + m) & 127), jnp.logical_and(m >= 0, m < 6))
            pick[c].append(jnp.where(hit, 1.0, 0.0))
        low = (lane_q - (y0 - 1)) & 255
        high = (lane_q + 128 - (y0 - 1)) & 255
        masks.append(jnp.concatenate(
            [jnp.where(low < 6, 1.0, 0.0), jnp.where(high < 6, 1.0, 0.0)], axis=1))
        later.append(jnp.broadcast_to((y0 & 4) != 0, (16, 128)))
    found = (dot_left_exact(jnp.concatenate(pick[0], axis=0), surface[0])
             + dot_left_exact(jnp.concatenate(pick[1], axis=0), surface[1]))
    found = found * jnp.concatenate(masks, axis=0)
    c_e = iota((256, 256), 0)
    l_e = iota((256, 256), 1)
    shift = jnp.where(l_e < 128, 1, 5)
    squeeze = jnp.where(((c_e + shift) & 7) == (l_e & 7), 1.0, 0.0)
    tight = dot_right_exact(found, squeeze)
    own_lanes = (lane_q >> 3) == k_q
    for q in range(Q):
        block = tight[16 * q:16 * q + 16]
        chosen = jnp.where(later[q], block[:, 128:], block[:, :128])
        rep_out[q // CAP, q % CAP:q % CAP + 1, :] = jnp.sum(
            jnp.where(own_lanes, chosen, 0.0), axis=0, keepdims=True)
    replies = [
        to_peer(-o, rep_out.at[o], rep_in.at[o], rep_send.at[o], rep_recv.at[o])
        for o in range(1, G)
    ]
    for copy in replies:
        copy.start()
    rep_in[0] = rep_out[0]

    asked_out[...] = req_in[...]
    for copy in halos:
        copy.wait_recv()
    ymix[...] = jnp.where(
        (iota((LZ, 128), 1) & 1) == 1, yth_in[1] * north_ok, yth_in[0] * south_ok)
    xhalo[0] = xth_in[0] * west_ok
    xhalo[1] = xth_in[1] * east_ok

    for copy in replies:
        copy.wait_recv()
    answers = jnp.concatenate([rep_in[o] for o in range(G)], axis=0)
    is_slot = jnp.where(code_col[:, :Q] == iota((TPD, Q), 1), 1.0, 0.0)
    patch = dot_left_exact(is_slot, answers)
    spread = jnp.concatenate(
        [jnp.where(own_lanes, patch[t:t + 1], 0.0) for t in range(TPD)], axis=0)
    by_y = jnp.where(
        (iota((128, 128), 0) & 7) < 6,
        interp_weight(iota((128, 128), 1), iota((128, 128), 0) & 7), 0.0)
    along_y = dot_right_exact(spread, by_y)
    high, middle, low = pieces(along_y)
    for t in range(TPD):
        small[t, 0:16, :] = high[16 * t:16 * t + 16]
        small[t, 16:32, :] = middle[16 * t:16 * t + 16]
        small[t, 32:48, :] = low[16 * t:16 * t + 16]

    for copy in requests + winds + halos + replies:
        copy.wait_send()


def fire(
    small, level_ref, fuel_ref, base, level_out, fuel_out, rows,
    wide, ping, pong, burn, wind, scaled,
):
    step = pl.program_id(0)
    lane_c = iota((R, 128), 1)
    first_lane = lane_c == 0
    last_lane = lane_c == 127

    @pl.when(step == 0)
    def _():
        fine_of = iota((2 * S, 48), 0)
        slot_of = iota((2 * S, 48), 1) & 15
        column = slot_of - 6 * (fine_of >> 7)
        wide[...] = jnp.where(
            jnp.logical_and(column >= 0, column < 6),
            interp_weight(fine_of & (S - 1), column), 0.0).astype(BF16)

    for p in range(PAIR):
        wind[p] = dot(wide[...], small[p])
        pong[p, 8:8 + S, :] = level_ref[0, 0, p]
        pong[p, 7:8, :] = level_ref[0, 0, p, 0:1, :]
        pong[p, 8 + S:9 + S, :] = level_ref[0, 0, p, S - 1:S, :]
        for b in range(S // R):
            strength = 0.015 * base[0, 0, p, R * b:R * b + R, :]
            scaled[p, R * b:R * b + R, :] = strength
            wind[p, R * b:R * b + R, :] = wind[p, R * b:R * b + R, :] * strength
            wind[p, S + R * b:S + R * b + R, :] = (
                wind[p, S + R * b:S + R * b + R, :] * strength)
    for k in range(KSUB):
        last = k == KSUB - 1
        for p in range(PAIR):
            old = (ping, pong)[(k - 1) % 2].at[p]
            new = (ping, pong)[k % 2].at[p]
            fuel_old = fuel_ref.at[0, 0, p] if k == 0 else burn.at[p]
            for b in range(S // R):
                at = 8 + R * b
                here_b = slice(R * b, R * b + R)
                centre = old[at:at + R, :]
                before = old[at - 1:at - 1 + R, :]
                after = old[at + 1:at + 1 + R, :]
                left = jnp.where(first_lane, centre, pltpu.roll(centre, 1, 1))
                right = jnp.where(last_lane, centre, pltpu.roll(centre, 127, 1))
                dx = after - before
                dy = right - left
                around = (after + before) + (right + left)
                square = (dx * dx + 0.04) + dy * dy
                length = square * lax.rsqrt(square)
                blown = (wind[p, R * b:R * b + R, :] * dx
                         + wind[p, S + R * b:S + R * b + R, :] * dy)
                rate = jnp.maximum(scaled[p, here_b, :] * length + blown, 0.0)
                level = (0.4 * centre + 0.15 * around) - rate
                fuel = fuel_old[here_b, :] * (0.925 + 0.075 * jnp.tanh(level))
                if last:
                    level_out[0, 0, p, here_b, :] = level
                    fuel_out[0, 0, p, here_b, :] = fuel
                    burnt = fuel_ref[0, 0, p, here_b, :] - fuel
                    rows[b, pl.ds(step * PAIR + p, 1), :] = jnp.sum(burnt, axis=0, keepdims=True)
                else:
                    new[at:at + R, :] = level
                    if b == 0:
                        new[7:8, :] = level[0:1]
                    if b == S // R - 1:
                        new[8 + S:9 + S, :] = level[R - 1:R]
                    burn[p, here_b, :] = fuel


def gather(
    G, LZ,
    theta_hbm, u_hbm, v_hbm, rows, code_row, req_in, ymix, xhalo,
    part_hbm, field_ref,
    th, uu, vv, part, flux_out, flux_in,
    in_sem, part_sem, flux_send, flux_recv,
):
    Q = G * CAP
    i = lax.axis_index("gx")
    j = lax.axis_index("gy")
    groups = LZ // GROUP
    lane = iota((8, 128), 1)
    sub = iota((8, 128), 0)

    def gx(offset):
        return lax.rem(i + (offset % G), G)

    barrier = pltpu.get_barrier_semaphore()
    for o in range(1, G):
        pl.semaphore_signal(barrier, inc=1, device_id=(gx(o), j), device_id_type=MESH)

    def arrays(zz):
        levels = pl.ds(zz * GROUP, GROUP)
        return [
            pltpu.make_async_copy(
                theta_hbm.at[levels], th.at[levels, 8:8 + BX, :], in_sem.at[0, zz]),
            pltpu.make_async_copy(u_hbm.at[levels], uu.at[levels], in_sem.at[1, zz]),
            pltpu.make_async_copy(v_hbm.at[levels], vv.at[levels], in_sem.at[2, zz]),
        ]

    for zz in range(groups):
        for load in arrays(zz):
            load.start()

    def to_peer(o, out, into, send, recv):
        return pltpu.make_async_remote_copy(
            src_ref=out, dst_ref=into, send_sem=send, recv_sem=recv,
            device_id=(gx(o), j), device_id_type=MESH)

    def unpack(mixed, n):
        return pltpu.roll(mixed, (127 - 2 * n) % 128, 1)

    l_m = iota((128, 128), 0)
    c_m = iota((128, 128), 1)
    mean = jnp.where((l_m >> 5) == (c_m & 3), 1.0 / (R * R), 0.0)
    fluxes = dot_right_exact(jnp.concatenate([rows[b] for b in range(TA)], axis=0), mean)
    slot_rows = iota((Q * TA, 64), 0)
    slot_lanes = iota((Q * TA, 64), 1)
    to_slot = jnp.where(
        jnp.logical_and(code_row[0:1, 0:64] == (slot_rows >> 2),
                        (slot_lanes >> 4) == (slot_rows & 3)), 1.0, 0.0)
    sent = dot_left_exact(to_slot, fluxes)
    for o in range(G):
        flux_out[o] = sent[8 * o:8 * o + 8]
    pl.semaphore_wait(barrier, G - 1)
    returned = [
        to_peer(o, flux_out.at[o], flux_in.at[o], flux_send.at[o], flux_recv.at[o])
        for o in range(1, G)
    ]
    for copy in returned:
        copy.start()
    flux_in[0] = flux_out[0]

    def advect(zz, carry):
        rows_of = pl.ds(pl.multiple_of(zz * 8, 8), 8)
        for load in arrays(zz):
            load.wait()
        mixed = ymix[rows_of, :]
        for zl in range(GROUP):
            z = zz * GROUP + zl
            th[z, 7:8, :] = xhalo[0, pl.ds(z, 1), :]
            th[z, 8 + BX:9 + BX, :] = xhalo[1, pl.ds(z, 1), :]
        for zl in range(GROUP):
            z = zz * GROUP + zl
            for g in range(8):
                at = 8 + 8 * g
                centre = th[z, at:at + 8, :]
                before = th[z, at - 1:at + 7, :]
                after = th[z, at + 1:at + 9, :]
                edge = unpack(mixed, zl * 8 + g)
                south = pltpu.roll(jnp.where(lane == 127, edge, centre), 1, 1)
                north = pltpu.roll(jnp.where(lane == 0, edge, centre), 127, 1)
                u = uu[z, 8 * g:8 * g + 8, :]
                v = vv[z, 8 * g:8 * g + 8, :]
                total = (jnp.maximum(u, 0.0) * (centre - before)
                         + jnp.minimum(u, 0.0) * (after - centre)
                         + jnp.maximum(v, 0.0) * (centre - south)
                         + jnp.minimum(v, 0.0) * (north - centre))
                part[z, 8 * g:8 * g + 8, :] = centre - 0.4 * total
        store(zz).start()
        return carry

    def store(zz):
        levels = pl.ds(zz * GROUP, GROUP)
        return pltpu.make_async_copy(part.at[levels], part_hbm.at[levels], part_sem.at[zz])

    lax.fori_loop(0, groups, advect, 0)

    lane8 = lane
    row8 = sub
    where_x = []
    where_y = []
    for o in range(G):
        p0 = req_in[o, 0:1, :].astype(jnp.int32)
        p1 = req_in[o, 1:2, :].astype(jnp.int32)
        place = jnp.where(row8 < TA, p0, p1)
        x0 = (place >> 5) * TA
        where_x.append(jnp.where(lane8 == x0 + (row8 & 3), 1.0, 0.0))
        where_y.append((lane8 >> 2) == (place & 31))
    across = jnp.concatenate(where_x, axis=0).T
    for copy in returned:
        copy.wait_recv()
    values = jnp.concatenate(
        [jnp.where(where_y[o], flux_in[o], 0.0) for o in range(G)], axis=0)
    field_ref[...] = dot_left_exact(across, values)[:BX]

    for copy in returned:
        copy.wait_send()

    def finish_group(zz, carry):
        store(zz).wait()
        return carry

    lax.fori_loop(0, groups, finish_group, 0)


def body(G, H, theta, wind_u, wind_v, level_set, fuel_load, spread_base, tile_owner, tile_place):
    LZ = theta.shape[0]
    assert theta.shape[1:] == (BX, BY) and level_set.shape[2:] == (TPD, S, S)
    far = pl.BlockSpec(memory_space=pl.ANY)
    vmem = pl.BlockSpec(memory_space=pltpu.VMEM)
    dma = pltpu.SemaphoreType.DMA
    shape = jax.ShapeDtypeStruct
    small, code, asked, ymix, xhalo = pl.pallas_call(
        functools.partial(exchange, G, H, LZ),
        out_shape=(
            shape((TPD, 48, S), BF16),
            shape((8, 128), jnp.int32),
            shape((G, 4, 128), F32),
            shape((LZ, 128), F32),
            shape((2, LZ, 128), F32),
        ),
        in_specs=[far] * 5,
        out_specs=(vmem,) * 5,
        scratch_shapes=[
            pltpu.VMEM((LZ, BX, BY), F32),
            pltpu.VMEM((BX, BY), F32),
            pltpu.VMEM((BX, BY), F32),
            pltpu.VMEM((TPD, 128), jnp.int32),
            pltpu.SMEM((1, 1, TPD), jnp.int32),
            pltpu.SMEM((1, 1, TPD), jnp.int32),
            pltpu.VMEM((G, 4, 128), F32),
            pltpu.VMEM((G, 4, 128), F32),
            pltpu.VMEM((G, 2, 128), F32),
            pltpu.VMEM((G, 2, 128), F32),
            pltpu.VMEM((8, 128), F32),
            pltpu.VMEM((6, 8, 128), F32),
            pltpu.VMEM((LZ, 128), F32),
            pltpu.VMEM((2, LZ, 128), F32),
            pltpu.VMEM((2, LZ, 128), F32),
            pltpu.VMEM((2, LZ, 128), F32),
            dma((5,)),
            dma((G,)), dma((G,)), dma((G,)), dma((G,)),
            dma((6,)), dma((6,)), dma((4,)), dma((4,)),
        ],
        compiler_params=pltpu.CompilerParams(
            collective_id=0, has_side_effects=True, vmem_limit_bytes=LIMITS[0] * 1024 * 1024),
    )(theta, wind_u, wind_v, tile_owner, tile_place)

    steps = TPD // PAIR
    tiles = pl.BlockSpec((1, 1, PAIR, S, S), lambda n: (0, 0, n, 0, 0))
    level_next, fuel_next, rows = pl.pallas_call(
        fire,
        grid=(steps,),
        out_shape=(
            shape(level_set.shape, F32),
            shape(level_set.shape, F32),
            shape((TA, TPD, S), F32),
        ),
        in_specs=[pl.BlockSpec((PAIR, 48, S), lambda n: (n, 0, 0)), tiles, tiles, tiles],
        out_specs=(tiles, tiles, pl.BlockSpec((TA, TPD, S), lambda n: (0, 0, 0))),
        scratch_shapes=[
            pltpu.VMEM((2 * S, 48), BF16),
            pltpu.VMEM((PAIR, S + 16, S), F32),
            pltpu.VMEM((PAIR, S + 16, S), F32),
            pltpu.VMEM((PAIR, S, S), F32),
            pltpu.VMEM((PAIR, 2 * S, S), F32),
            pltpu.VMEM((PAIR, S, S), F32),
        ],
        compiler_params=pltpu.CompilerParams(vmem_limit_bytes=LIMITS[1] * 1024 * 1024),
    )(small, level_set, fuel_load, spread_base)

    groups = LZ // GROUP
    part, field = pl.pallas_call(
        functools.partial(gather, G, LZ),
        out_shape=(shape(theta.shape, F32), shape((BX, BY), F32)),
        in_specs=[far] * 3 + [vmem] * 5,
        out_specs=(far, vmem),
        scratch_shapes=[
            pltpu.VMEM((LZ, BX + 16, BY), F32),
            pltpu.VMEM((LZ, BX, BY), F32),
            pltpu.VMEM((LZ, BX, BY), F32),
            pltpu.VMEM((LZ, BX, BY), F32),
            pltpu.VMEM((G, 8, 128), F32),
            pltpu.VMEM((G, 8, 128), F32),
            dma((3, groups)), dma((groups,)), dma((G,)), dma((G,)),
        ],
        compiler_params=pltpu.CompilerParams(
            collective_id=1, has_side_effects=True, vmem_limit_bytes=LIMITS[2] * 1024 * 1024),
    )(theta, wind_u, wind_v, rows, code, asked, ymix, xhalo)
    profile = 2.0 * jnp.exp(-(jnp.arange(LZ, dtype=F32) + 0.5) / (LZ / 4.0))
    theta_next = part + field[None, :, :] * profile[:, None, None]
    return (theta_next, level_next, fuel_next)


def solution(mesh):
    columns = P(None, "gx", "gy")
    tiles = P("gx", "gy", None, None, None)
    lists = P("gx", "gy", None)
    return jax.shard_map(
        functools.partial(body, mesh.shape["gx"], mesh.shape["gy"]),
        mesh=mesh,
        in_specs=(columns, columns, columns, tiles, tiles, tiles, lists, lists),
        out_specs=(columns, tiles, tiles),
        check_vma=False,
    )
```

time: 52.2 us -> 48.6 us (0.931)
  local copies, waits for them, and re-layouts: 10.4 us -> 4.8 us
  Pallas kernels: 39 us -> 41.1 us
    unnamed x16, local copies, waits for them, and re-layouts: 10.4 us -> 4.8 us
    pallas_call x1 -> x3, Pallas kernels: 39 us -> 41.1 us  [the longest x1 16.8 us: body(): pl.pallas_call(functools.partial(exchange, G, H, LZ), out_shape=(shape((T...]
where the time goes in v3:
time: 48.6 us; the launch traced here: 48.4 us
  Pallas kernels  41.1 us (85%)
  local copies, waits for them, and re-layouts  4.8 us (10%)
  other arithmetic  1.79 us (4%)
  between operations  0.69 us (1%)
    pallas_call x1, Pallas kernels, body(): pl.pallas_call(functools.partial(exchange, G, H, LZ), out_shape=(shape((T...  16.8 us
    pallas_call x1, Pallas kernels, body(): pl.pallas_call(functools.partial(gather, G, LZ), out_shape=(shape(theta.s...  16.4 us
    pallas_call x1, Pallas kernels, body(): pl.pallas_call(fire, grid=(steps,), out_shape=(shape(level_set.shape, F32...  7.98 us
    unnamed x16, local copies, waits for them, and re-layouts  4.8 us
    add x1, other arithmetic, body(): theta_next = part + field[None, :, :] * profile[:, None, None]  1.77 us

profile of v3, /device:TPU:0, one launch (start us, length us, event | category | flops | bytes accessed | tf_op | source)
XLA Modules:
  0.0 48.4 jit_solution(3078816903844547650)
XLA Ops:
  0.6 0.0 copy-start
  0.7 1.7 %copy-done = f32[80,64,128]{2,1,0:T(8,128)S(1)} copy-done((f32[80,64,128]{2,1,0:T(8,128)S(1)}, f32[80,64,128]{2,1,0:T(8,128)}, u32[]{:S(2)}) %copy-start) | copy-done | bytes 2621464
  2.4 0.0 copy-start.1
  2.4 1.7 %copy-done.1 = f32[80,64,128]{2,1,0:T(8,128)S(1)} copy-done((f32[80,64,128]{2,1,0:T(8,128)S(1)}, f32[80,64,128]{2,1,0:T(8,128)}, u32[]{:S(2)}) %copy-start.1) | copy-done | bytes 2621464
  4.1 0.0 copy-start.6
  4.1 0.7 %copy-done.6 = s32[1,1,16]{2,1,0:T(1,128)S(1)} copy-done((s32[1,1,16]{2,1,0:T(1,128)S(1)}, s32[1,1,16]{2,1,0:T(1,128)}, u32[]{:S(2)}) %copy-start.6) | copy-done | bytes 88
  4.8 0.0 copy-start.7
  4.8 0.7 %copy-done.7 = s32[1,1,16]{2,1,0:T(1,128)S(1)} copy-done((s32[1,1,16]{2,1,0:T(1,128)S(1)}, s32[1,1,16]{2,1,0:T(1,128)}, u32[]{:S(2)}) %copy-start.7) | copy-done | bytes 88
  5.4 0.0 copy-start.3
  5.4 0.0 copy-start.4
  5.4 0.0 copy-start.5
  5.4 16.8 %shard_map.103 = (bf16[16,48,128]{2,1,0:T(8,128)(2,1)S(1)}, s32[8,128]{1,0:T(8,128)S(1)}, f32[8,4,128]{2,1,0:T(4,128)S(1)}, f32[80,128]{1,0:T(8,128)S(1)}, f32[2,80,128]{2,1,0:T(8,128)S(1)}) custom-call(f32[80,64,128]{2,1,0:T(8,128)S(1)} %copy-done, f32[80,64,128]{2,1,0:T(8,128)S(1)} %copy-done.1, f32[80,64,128]{2,1,0:T(8,128)} %v_hbm.3, ...), custom_call_target="tpu_custom_call" | custom-call | tf_op jit(solution)/shard_map/pallas_call | solution.py:504
  22.2 0.0 copy-start.2
  22.3 0.0 copy-done.3
  22.3 0.0 copy-done.4
  22.3 0.0 copy-done.5
  22.3 8.0 %shard_map.104 = (f32[1,1,16,128,128]{4,3,2,1,0:T(8,128)}, f32[1,1,16,128,128]{4,3,2,1,0:T(8,128)}, f32[4,16,128]{2,1,0:T(8,128)S(1)}) custom-call(bf16[16,48,128]{2,1,0:T(8,128)(2,1)S(1)} %get-tuple-element.13.small, f32[1,1,16,128,128]{4,3,2,1,0:T(8,128)S(1)} %copy-done.3, f32[1,1,16,128,128]{4,3,2,1,0:T(8,128)S(1)} %copy-done.4, ...), custom_call_target="tpu_custom_call" | custom-call | tf_op jit(solution)/shard_map/pallas_call | solution.py:542
  30.3 0.0 copy-done.2
  30.3 16.4 %shard_map.105 = (f32[80,64,128]{2,1,0:T(8,128)S(1)}, f32[64,128]{1,0:T(8,128)S(1)}) custom-call(f32[80,64,128]{2,1,0:T(8,128)S(1)} %copy-done, f32[80,64,128]{2,1,0:T(8,128)S(1)} %copy-done.1, f32[80,64,128]{2,1,0:T(8,128)S(1)} %copy-done.2, f32[4,16,128]{2,1,0:T(8,128)S(1)} %get-tuple-element.14.rows, s32[8,128]{1,0:T(8,128)S(1)} %get-tuple-element.15.code_row, ...), custom_call_target="tpu_custom_call" | custom-call | tf_op jit(solution)/shard_map/pallas_call | solution.py:564
  46.6 1.8 %multiply_add_fusion = f32[80,64,128]{2,1,0:T(8,128)} fusion(f32[80,64,128]{2,1,0:T(8,128)S(1)} %get-tuple-element.19, f32[80]{0:T(128)S(1)} %exponential_multiply_fusion, f32[64,128]{1,0:T(8,128)S(1)} %get-tuple-element.20), kind=kLoop, calls=%fused_computation | loop fusion | flops 1310720 | bytes 5275968 | tf_op jit(solution)/shard_map/add | solution.py:582
  (1 shorter events, 0.0 us)
Async XLA Ops:
  0.6 1.7 %copy-start = (f32[80,64,128]{2,1,0:T(8,128)S(1)}, f32[80,64,128]{2,1,0:T(8,128)}, u32[]{:S(2)}) copy-start(f32[80,64,128]{2,1,0:T(8,128)} %theta_hbm.3) | copy-start | bytes 7864324
  2.4 1.7 %copy-start.1 = (f32[80,64,128]{2,1,0:T(8,128)S(1)}, f32[80,64,128]{2,1,0:T(8,128)}, u32[]{:S(2)}) copy-start(f32[80,64,128]{2,1,0:T(8,128)} %u_hbm.3) | copy-start | bytes 7864324
  4.1 0.7 %copy-start.6 = (s32[1,1,16]{2,1,0:T(1,128)S(1)}, s32[1,1,16]{2,1,0:T(1,128)}, u32[]{:S(2)}) copy-start(s32[1,1,16]{2,1,0:T(1,128)} %owner_hbm.1) | copy-start | bytes 196
  4.8 0.7 %copy-start.7 = (s32[1,1,16]{2,1,0:T(1,128)S(1)}, s32[1,1,16]{2,1,0:T(1,128)}, u32[]{:S(2)}) copy-start(s32[1,1,16]{2,1,0:T(1,128)} %place_hbm.1) | copy-start | bytes 196
  5.4 16.8 %copy-start.3 = (f32[1,1,16,128,128]{4,3,2,1,0:T(8,128)S(1)}, f32[1,1,16,128,128]{4,3,2,1,0:T(8,128)}, u32[]{:S(2)}) copy-start(f32[1,1,16,128,128]{4,3,2,1,0:T(8,128)} %level_ref.1) | copy-start | bytes 3145732
  5.4 16.8 %copy-start.4 = (f32[1,1,16,128,128]{4,3,2,1,0:T(8,128)S(1)}, f32[1,1,16,128,128]{4,3,2,1,0:T(8,128)}, u32[]{:S(2)}) copy-start(f32[1,1,16,128,128]{4,3,2,1,0:T(8,128)} %fuel_ref.1) | copy-start | bytes 3145732
  5.4 16.8 %copy-start.5 = (f32[1,1,16,128,128]{4,3,2,1,0:T(8,128)S(1)}, f32[1,1,16,128,128]{4,3,2,1,0:T(8,128)}, u32[]{:S(2)}) copy-start(f32[1,1,16,128,128]{4,3,2,1,0:T(8,128)} %base.1) | copy-start | bytes 3145732
  22.2 8.0 %copy-start.2 = (f32[80,64,128]{2,1,0:T(8,128)S(1)}, f32[80,64,128]{2,1,0:T(8,128)}, u32[]{:S(2)}) copy-start(f32[80,64,128]{2,1,0:T(8,128)} %v_hbm.3) | copy-start | bytes 7864324

commit v4 on v2

--- a/solution.py
+++ b/solution.py
@@ -57,10 +57,10 @@
 
 def kernel(
     G, H, LZ,
-    theta_hbm, u_hbm, v_hbm, level_hbm, fuel_hbm, base_hbm, owner_hbm, place_hbm,
+    theta_hbm, u_hbm, v_hbm, level_hbm, fuel_hbm, base_hbm, lists_hbm,
     part_hbm, level_out, fuel_out, field_ref,
     th, uu, vv, part, lev, lout, ping, pong, fin, burn, fout, base, wind, scaled,
-    wide, small, rows, code_col, owner_ref, place_ref,
+    wide, small, rows, code_col, lists,
     req_out, req_in, rep_out, rep_in, flux_out, flux_in,
     yw_out, yw_in, yth_out, yth_in, xth_out, xth_in,
     in_sem, lev_sem, fuel_sem, part_sem,
@@ -78,8 +78,7 @@
         return lax.rem(j + (offset % H), H)
 
     loads = [
-        pltpu.make_async_copy(owner_hbm, owner_ref, in_sem.at[8]),
-        pltpu.make_async_copy(place_hbm, place_ref, in_sem.at[9]),
+        pltpu.make_async_copy(lists_hbm, lists, in_sem.at[8]),
         pltpu.make_async_copy(u_hbm.at[0], uu.at[0], in_sem.at[0]),
         pltpu.make_async_copy(v_hbm.at[0], vv.at[0], in_sem.at[1]),
         pltpu.make_async_copy(theta_hbm, th.at[:, 8:8 + BX, :], in_sem.at[2]),
@@ -100,7 +99,6 @@
         pl.semaphore_signal(barrier, inc=1, device_id=(gx(dx), gy(dy)), device_id_type=MESH)
 
     loads[0].wait()
-    loads[1].wait()
     lane = iota((8, 128), 1)
     lane16 = lane & (TPD - 1)
     sub16 = iota((TPD, 128), 0)
@@ -108,16 +106,16 @@
     place_row = jnp.zeros((8, 128), jnp.int32)
     own_col = jnp.zeros((TPD, 128), jnp.int32)
     for t in range(TPD):
-        own_row = jnp.where(lane16 == t, owner_ref[0, 0, t], own_row)
-        place_row = jnp.where(lane16 == t, place_ref[0, 0, t], place_row)
-        own_col = jnp.where(sub16 == t, owner_ref[0, 0, t], own_col)
+        own_row = jnp.where(lane16 == t, lists[0, 0, t], own_row)
+        place_row = jnp.where(lane16 == t, lists[0, 1, t], place_row)
+        own_col = jnp.where(sub16 == t, lists[0, 0, t], own_col)
     rank_row = jnp.zeros((8, 128), jnp.int32)
     rank_col = jnp.zeros((TPD, 128), jnp.int32)
     for t in range(TPD):
         rank_row += jnp.where(
-            jnp.logical_and(own_row == owner_ref[0, 0, t], lane16 > t), 1, 0)
+            jnp.logical_and(own_row == lists[0, 0, t], lane16 > t), 1, 0)
         rank_col += jnp.where(
-            jnp.logical_and(own_col == owner_ref[0, 0, t], sub16 > t), 1, 0)
+            jnp.logical_and(own_col == lists[0, 0, t], sub16 > t), 1, 0)
 
     def code_of(owner, rank):
         away = owner - i
@@ -133,8 +131,8 @@
         place1 + 1, 0).astype(F32)
     asked = jnp.broadcast_to(jnp.sum(wanted, axis=1, keepdims=True) - 1.0, (Q, 128))
 
+    loads[1].wait()
     loads[2].wait()
-    loads[3].wait()
     for o in range(G):
         req_out[o, 0:2, :] = asked[2 * o:2 * o + 2]
         edge = 0 if o == G - 1 else BX - 1
@@ -176,19 +174,29 @@
         interp_weight(fine_of & (S - 1), column), 0.0).astype(BF16)
     wide[...] = a3
 
-    loads[4].wait()
+    loads[3].wait()
 
     def pack(zz, carry):
-        acc = jnp.zeros((8, 128), F32)
+        parts = []
         for zl in range(GROUP):
             z = zz * GROUP + zl
+            acc = jnp.zeros((8, 128), F32)
             for g in range(8):
                 n = zl * 8 + g
                 cell = th[z, 8 + 8 * g:16 + 8 * g, :]
                 acc = jnp.where((lane >> 1) == n, pltpu.roll(cell, (2 * n + 1) % 128, 1), acc)
-            xth_out[0, pl.ds(z, 1), :] = th[z, 7 + BX:8 + BX, :]
-            xth_out[1, pl.ds(z, 1), :] = th[z, 8:9, :]
-        yth_out[pl.ds(pl.multiple_of(zz * 8, 8), 8), :] = acc
+            parts.append(acc)
+        while len(parts) > 1:
+            parts = [parts[n] + parts[n + 1] for n in range(0, len(parts), 2)]
+        acc = parts[0]
+        levels = range(GROUP)
+        low = jnp.concatenate([th[zz * GROUP + zl, 8:9, :] for zl in levels], axis=0)
+        high = jnp.concatenate(
+            [th[zz * GROUP + zl, 7 + BX:8 + BX, :] for zl in levels], axis=0)
+        rows_of = pl.ds(pl.multiple_of(zz * 8, 8), 8)
+        xth_out[0, rows_of, :] = high
+        xth_out[1, rows_of, :] = low
+        yth_out[rows_of, :] = acc
         return carry
 
     lax.fori_loop(0, LZ // GROUP, pack, 0)
@@ -288,23 +296,26 @@
     def advect(zz, carry):
         rows_of = pl.ds(pl.multiple_of(zz * 8, 8), 8)
         mixed = both(yth_in[0, rows_of, :], yth_in[1, rows_of, :])
-        for zl in range(GROUP):
-            z = zz * GROUP + zl
-            for g in range(8):
-                at = 8 + 8 * g
-                centre = th[z, at:at + 8, :]
-                before = th[z, at - 1:at + 7, :]
-                after = th[z, at + 1:at + 9, :]
-                edge = unpack(mixed, zl * 8 + g)
-                south = pltpu.roll(jnp.where(lane == 127, edge, centre), 1, 1)
-                north = pltpu.roll(jnp.where(lane == 0, edge, centre), 127, 1)
-                u = uu[z, 8 * g:8 * g + 8, :]
-                v = vv[z, 8 * g:8 * g + 8, :]
+        lane_x = iota((BX, 128), 1)
+        for first in range(0, GROUP, 2):
+            done = []
+            for zl in (first, first + 1):
+                z = zz * GROUP + zl
+                centre = th[z, 8:8 + BX, :]
+                before = th[z, 7:7 + BX, :]
+                after = th[z, 9:9 + BX, :]
+                edge = jnp.concatenate([unpack(mixed, zl * 8 + g) for g in range(8)], axis=0)
+                south = pltpu.roll(jnp.where(lane_x == 127, edge, centre), 1, 1)
+                north = pltpu.roll(jnp.where(lane_x == 0, edge, centre), 127, 1)
+                u = uu[z]
+                v = vv[z]
                 total = (jnp.maximum(u, 0.0) * (centre - before)
                          + jnp.minimum(u, 0.0) * (after - centre)
                          + jnp.maximum(v, 0.0) * (centre - south)
                          + jnp.minimum(v, 0.0) * (north - centre))
-                part[z, 8 * g:8 * g + 8, :] = centre - 0.4 * total
+                done.append((z, centre - 0.4 * total))
+            for z, value in done:
+                part[z] = value
         store(zz).start()
         return carry
 
@@ -316,14 +327,17 @@
     first_groups = groups // 2
     for copy in halos:
         copy.wait_recv()
+    loads[4].wait()
     loads[5].wait()
-    loads[6].wait()
 
     def rim(zz, carry):
+        rows_of = pl.ds(pl.multiple_of(zz * 8, 8), 8)
+        low = xth_in[0, rows_of, :] * west_ok
+        high = xth_in[1, rows_of, :] * east_ok
         for zl in range(GROUP):
             z = zz * GROUP + zl
-            th[z, 7:8, :] = xth_in[0, pl.ds(z, 1), :] * west_ok
-            th[z, 8 + BX:9 + BX, :] = xth_in[1, pl.ds(z, 1), :] * east_ok
+            th[z, 7:8, :] = low[zl:zl + 1]
+            th[z, 8 + BX:9 + BX, :] = high[zl:zl + 1]
         return carry
 
     lax.fori_loop(0, groups, rim, 0)
@@ -346,7 +360,7 @@
         small[t, 16:32, :] = middle[16 * t:16 * t + 16]
         small[t, 32:48, :] = low[16 * t:16 * t + 16]
 
-    for load in loads[7:]:
+    for load in loads[6:]:
         load.wait()
     pair = 2
     lane_c = iota((R, 128), 1)
@@ -478,19 +492,6 @@
     lax.fori_loop(0, groups, finish_group, 0)
 
 
-def finish(LZ, per_step, part, level, fuel, field, theta_next, level_next, fuel_next):
-    first = pl.program_id(0) * per_step
-    heat = 2.0 * field[...]
-    for n in range(per_step):
-        z = jnp.full((8, BY), first + n, jnp.int32).astype(F32)
-        profile = jnp.exp(-(z + 0.5) / (LZ / 4.0))
-        for g in range(BX // 8):
-            at = slice(8 * g, 8 * g + 8)
-            theta_next[n, at, :] = part[n, at, :] + heat[at] * profile
-    level_next[...] = level[...]
-    fuel_next[...] = fuel[...]
-
-
 def body(G, H, theta, wind_u, wind_v, level_set, fuel_load, spread_base, tile_owner, tile_place):
     LZ = theta.shape[0]
     assert theta.shape[1:] == (BX, BY) and level_set.shape[2:] == (TPD, S, S)
@@ -517,8 +518,7 @@
         pltpu.VMEM((TPD, 48, S), BF16),
         pltpu.VMEM((TA, TPD, S), F32),
         pltpu.VMEM((TPD, 128), jnp.int32),
-        pltpu.SMEM((1, 1, TPD), jnp.int32),
-        pltpu.SMEM((1, 1, TPD), jnp.int32),
+        pltpu.SMEM((1, 2, TPD), jnp.int32),
         pltpu.VMEM((G, 4, 128), F32),
         pltpu.VMEM((G, 4, 128), F32),
         pltpu.VMEM((G, 2, 128), F32),
@@ -531,7 +531,7 @@
         pltpu.VMEM((2, LZ, 128), F32),
         pltpu.VMEM((2, LZ, 128), F32),
         pltpu.VMEM((2, LZ, 128), F32),
-        dma((10,)), dma((TPD,)), dma((TPD,)), dma((LZ // GROUP,)),
+        dma((9,)), dma((TPD,)), dma((TPD,)), dma((LZ // GROUP,)),
         dma((G,)), dma((G,)), dma((G,)), dma((G,)), dma((G,)), dma((G,)),
         dma((6,)), dma((6,)), dma((4,)), dma((4,)),
     ]
@@ -543,28 +543,16 @@
             jax.ShapeDtypeStruct(level_set.shape, F32),
             jax.ShapeDtypeStruct((BX, BY), F32),
         ),
-        in_specs=[far] * 8,
+        in_specs=[far] * 7,
         out_specs=(anywhere, anywhere, anywhere, vmem),
         scratch_shapes=scratch,
         compiler_params=pltpu.CompilerParams(
-            collective_id=0, has_side_effects=True, vmem_limit_bytes=58 * 1024 * 1024),
-    )(theta, wind_u, wind_v, level_set, fuel_load, spread_base, tile_owner, tile_place)
-    steps = 8
-    levels = pl.BlockSpec((LZ // steps, BX, BY), lambda n: (n, 0, 0))
-    two = pl.BlockSpec((1, 1, TPD // steps, S, S), lambda n: (0, 0, n, 0, 0))
-    whole = pl.BlockSpec((BX, BY), lambda n: (0, 0))
-    return pl.pallas_call(
-        functools.partial(finish, LZ, LZ // steps),
-        grid=(steps,),
-        out_shape=(
-            jax.ShapeDtypeStruct(theta.shape, F32),
-            jax.ShapeDtypeStruct(level_set.shape, F32),
-            jax.ShapeDtypeStruct(level_set.shape, F32),
-        ),
-        in_specs=[levels, two, two, whole],
-        out_specs=(levels, two, two),
-        compiler_params=pltpu.CompilerParams(vmem_limit_bytes=58 * 1024 * 1024),
-    )(part, level_next, fuel_next, field)
+            collective_id=0, has_side_effects=True, vmem_limit_bytes=51 * 1024 * 1024),
+    )(theta, wind_u, wind_v, level_set, fuel_load, spread_base,
+      jnp.concatenate([tile_owner, tile_place], axis=1))
+    profile = 2.0 * jnp.exp(-(jnp.arange(LZ, dtype=F32) + 0.5) / (LZ / 4.0))
+    theta_next = part + field[None, :, :] * profile[:, None, None]
+    return (theta_next, level_next, fuel_next)
 
 
 def solution(mesh):

time: 43.2 us -> 37.8 us (0.87)
  Pallas kernels: 42.2 us -> 30.8 us
  other arithmetic: 0 us -> 4.21 us
  local copies, waits for them, and re-layouts: 0 us -> 1.94 us
    pallas_call x1 -> x0, Pallas kernels: 6.82 us -> none  [body(): pl.pallas_call(functools.partial(finish, LZ, LZ // steps), grid=(steps,),...]
    pallas_call x1, Pallas kernels: 35.4 us -> 30.8 us  [body(): pl.pallas_call(functools.partial(kernel, G, H, LZ), out_shape=(jax.ShapeD...]
    add x0 -> x1, other arithmetic: none -> 3.51 us  [body(): theta_next = part + field[None, :, :] * profile[:, None, None]]
    unnamed x0 -> x2, local copies, waits for them, and re-layouts: none -> 1.94 us
    concatenate x0 -> x1, other arithmetic: none -> 0.68 us  [body(): jnp.concatenate([tile_owner, tile_place], axis=1)]
where the time goes in v4:
time: 37.8 us; the launch traced here: 37.6 us
  Pallas kernels  30.8 us (81%)
  other arithmetic  4.21 us (11%)
  local copies, waits for them, and re-layouts  1.94 us (5%)
  between operations  0.64 us (2%)
    pallas_call x1, Pallas kernels, body(): pl.pallas_call(functools.partial(kernel, G, H, LZ), out_shape=(jax.ShapeD...  30.8 us
    add x1, other arithmetic, body(): theta_next = part + field[None, :, :] * profile[:, None, None]  3.51 us
    unnamed x2, local copies, waits for them, and re-layouts  1.94 us

profile of v4, /device:TPU:0, one launch (start us, length us, event | category | flops | bytes accessed | tf_op | source)
XLA Modules:
  0.0 37.6 jit_solution(8904296779269172350)
XLA Ops:
  0.6 0.7 %pad_add_fusion.lists_hbm = s32[1,2,16]{2,1,0:T(2,128)S(1)} fusion(s32[1,1,16]{2,1,0:T(1,128)} %param.15, s32[1,1,16]{2,1,0:T(1,128)} %param.14), kind=kLoop, calls=%fused_computation.1 | loop fusion | flops 32 | bytes 256 | tf_op jit(solution)/shard_map/concatenate | solution.py:552
  1.3 30.8 %shard_map.103 = (f32[80,64,128]{2,1,0:T(8,128)}, f32[1,1,16,128,128]{4,3,2,1,0:T(8,128)S(1)}, f32[1,1,16,128,128]{4,3,2,1,0:T(8,128)S(1)}, f32[64,128]{1,0:T(8,128)S(1)}) custom-call(f32[80,64,128]{2,1,0:T(8,128)} %theta_hbm.1, f32[80,64,128]{2,1,0:T(8,128)} %u_hbm.1, f32[80,64,128]{2,1,0:T(8,128)} %v_hbm.1, f32[1,1,16,128,128]{4,3,2,1,0:T(8,128)} %level_hbm.1, ...), custom_call_target="tpu_custom_call" | custom-call | tf_op jit(solution)/shard_map/pallas_call | solution.py:538
  32.2 3.5 %multiply_add_fusion = f32[80,64,128]{2,1,0:T(8,128)} fusion(f32[80,64,128]{2,1,0:T(8,128)} %get-tuple-element.7, f32[80]{0:T(128)S(1)} %exponential_multiply_fusion, f32[64,128]{1,0:T(8,128)S(1)} %get-tuple-element.8), kind=kLoop, calls=%fused_computation | loop fusion | flops 1310720 | bytes 5275968 | tf_op jit(solution)/shard_map/add | solution.py:554
  35.7 1.0 %copy.13 = f32[1,1,16,128,128]{4,3,2,1,0:T(8,128)} copy(f32[1,1,16,128,128]{4,3,2,1,0:T(8,128)S(1)} %get-tuple-element.15) | data formatting | bytes 2097152
  36.6 1.0 %copy.14 = f32[1,1,16,128,128]{4,3,2,1,0:T(8,128)} copy(f32[1,1,16,128,128]{4,3,2,1,0:T(8,128)S(1)} %get-tuple-element.16) | data formatting | bytes 2097152
  (1 shorter events, 0.0 us)

commit v5 on v4

--- a/solution.py
+++ b/solution.py
@@ -28,10 +28,7 @@
 
 def pieces(x):
     high = x.astype(BF16)
-    rest = x - high.astype(F32)
-    middle = rest.astype(BF16)
-    low = (rest - middle.astype(F32)).astype(BF16)
-    return (high, middle, low)
+    return (high, (x - high.astype(F32)).astype(BF16))
 
 
 def dot(a, b):
@@ -40,14 +37,14 @@
 
 def dot_left_exact(a, b):
     a = a.astype(BF16)
-    high, middle, low = pieces(b)
-    return dot(a, high) + (dot(a, middle) + dot(a, low))
+    high, low = pieces(b)
+    return dot(a, high) + dot(a, low)
 
 
 def dot_right_exact(a, b):
     b = b.astype(BF16)
-    high, middle, low = pieces(a)
-    return dot(high, b) + (dot(middle, b) + dot(low, b))
+    high, low = pieces(a)
+    return dot(high, b) + dot(low, b)
 
 
 def interp_weight(fine, column):
@@ -88,7 +85,7 @@
         pltpu.make_async_copy(fuel_hbm.at[0, 0], fin, in_sem.at[6]),
         pltpu.make_async_copy(base_hbm.at[0, 0], base, in_sem.at[7]),
     ]
-    for load in loads:
+    for load in loads[:4]:
         load.start()
 
     corners = [(0, 1), (0, -1), (-1, 1), (-1, -1), (1, 1), (1, -1)]
@@ -166,8 +163,8 @@
         copy.start()
     req_in[0] = req_out[0]
 
-    fine_of = iota((2 * S, 48), 0)
-    slot_of = iota((2 * S, 48), 1) & 15
+    fine_of = iota((2 * S, 32), 0)
+    slot_of = iota((2 * S, 32), 1) & 15
     column = slot_of - 6 * (fine_of >> 7)
     a3 = jnp.where(
         jnp.logical_and(column >= 0, column < 6),
@@ -175,6 +172,8 @@
     wide[...] = a3
 
     loads[3].wait()
+    for load in loads[4:6]:
+        load.start()
 
     def pack(zz, carry):
         parts = []
@@ -200,6 +199,8 @@
         return carry
 
     lax.fori_loop(0, LZ // GROUP, pack, 0)
+    for load in loads[6:]:
+        load.start()
     halos = []
     for n, (out, into, dx, dy) in enumerate([
         (xth_out.at[0], xth_in.at[0], 1, 0),
@@ -297,9 +298,9 @@
         rows_of = pl.ds(pl.multiple_of(zz * 8, 8), 8)
         mixed = both(yth_in[0, rows_of, :], yth_in[1, rows_of, :])
         lane_x = iota((BX, 128), 1)
-        for first in range(0, GROUP, 2):
+        for first in range(0, GROUP, 4):
             done = []
-            for zl in (first, first + 1):
+            for zl in range(first, first + 4):
                 z = zz * GROUP + zl
                 centre = th[z, 8:8 + BX, :]
                 before = th[z, 7:7 + BX, :]
@@ -354,11 +355,10 @@
         (iota((128, 128), 0) & 7) < 6,
         interp_weight(iota((128, 128), 1), iota((128, 128), 0) & 7), 0.0)
     along_y = dot_right_exact(spread, by_y)
-    high, middle, low = pieces(along_y)
+    high, low = pieces(along_y)
     for t in range(TPD):
         small[t, 0:16, :] = high[16 * t:16 * t + 16]
-        small[t, 16:32, :] = middle[16 * t:16 * t + 16]
-        small[t, 32:48, :] = low[16 * t:16 * t + 16]
+        small[t, 16:32, :] = low[16 * t:16 * t + 16]
 
     for load in loads[6:]:
         load.wait()
@@ -514,8 +514,8 @@
         pltpu.VMEM((TPD, S, S), F32),
         pltpu.VMEM((2, 2 * S, S), F32),
         pltpu.VMEM((2, S, S), F32),
-        pltpu.VMEM((2 * S, 48), BF16),
-        pltpu.VMEM((TPD, 48, S), BF16),
+        pltpu.VMEM((2 * S, 32), BF16),
+        pltpu.VMEM((TPD, 32, S), BF16),
         pltpu.VMEM((TA, TPD, S), F32),
         pltpu.VMEM((TPD, 128), jnp.int32),
         pltpu.SMEM((1, 2, TPD), jnp.int32),

time: 37.8 us -> 37.7 us (level)
  no operation moved by 1% of the time
where the time goes in v5:
time: 37.7 us; the launch traced here: 37.5 us
  Pallas kernels  30.7 us (81%)
  other arithmetic  4.21 us (11%)
  local copies, waits for them, and re-layouts  1.94 us (5%)
  between operations  0.64 us (2%)
    pallas_call x1, Pallas kernels, body(): pl.pallas_call(functools.partial(kernel, G, H, LZ), out_shape=(jax.ShapeD...  30.7 us
    add x1, other arithmetic, body(): theta_next = part + field[None, :, :] * profile[:, None, None]  3.51 us
    unnamed x2, local copies, waits for them, and re-layouts  1.94 us

profile of v5, /device:TPU:0, one launch (start us, length us, event | category | flops | bytes accessed | tf_op | source)
XLA Modules:
  0.0 37.5 jit_solution(556277079404237810)
XLA Ops:
  0.6 0.7 %pad_add_fusion.lists_hbm = s32[1,2,16]{2,1,0:T(2,128)S(1)} fusion(s32[1,1,16]{2,1,0:T(1,128)} %param.15, s32[1,1,16]{2,1,0:T(1,128)} %param.14), kind=kLoop, calls=%fused_computation.1 | loop fusion | flops 32 | bytes 256 | tf_op jit(solution)/shard_map/concatenate | solution.py:552
  1.3 30.7 %shard_map.103 = (f32[80,64,128]{2,1,0:T(8,128)}, f32[1,1,16,128,128]{4,3,2,1,0:T(8,128)S(1)}, f32[1,1,16,128,128]{4,3,2,1,0:T(8,128)S(1)}, f32[64,128]{1,0:T(8,128)S(1)}) custom-call(f32[80,64,128]{2,1,0:T(8,128)} %theta_hbm.1, f32[80,64,128]{2,1,0:T(8,128)} %u_hbm.1, f32[80,64,128]{2,1,0:T(8,128)} %v_hbm.1, f32[1,1,16,128,128]{4,3,2,1,0:T(8,128)} %level_hbm.1, ...), custom_call_target="tpu_custom_call" | custom-call | tf_op jit(solution)/shard_map/pallas_call | solution.py:538
  32.1 3.5 %multiply_add_fusion = f32[80,64,128]{2,1,0:T(8,128)} fusion(f32[80,64,128]{2,1,0:T(8,128)} %get-tuple-element.7, f32[80]{0:T(128)S(1)} %exponential_multiply_fusion, f32[64,128]{1,0:T(8,128)S(1)} %get-tuple-element.8), kind=kLoop, calls=%fused_computation | loop fusion | flops 1310720 | bytes 5275968 | tf_op jit(solution)/shard_map/add | solution.py:554
  35.6 1.0 %copy.13 = f32[1,1,16,128,128]{4,3,2,1,0:T(8,128)} copy(f32[1,1,16,128,128]{4,3,2,1,0:T(8,128)S(1)} %get-tuple-element.15) | data formatting | bytes 2097152
  36.5 1.0 %copy.14 = f32[1,1,16,128,128]{4,3,2,1,0:T(8,128)} copy(f32[1,1,16,128,128]{4,3,2,1,0:T(8,128)S(1)} %get-tuple-element.16) | data formatting | bytes 2097152
  (1 shorter events, 0.0 us)
